TPU v7x, 32 devices: a whole 2x2x4 slice. The times are simulated.
32 devices in a mesh: blk: 16 (over z, x, core), dp: 2 (over y).
Axes of the slice: x: 2, y: 2, z: 4, core: 2. Of those that a mesh axis runs over, the one named last changes fastest.
Arguments:
- tokens: bfloat16 [6144, 2048], P(('blk', 'dp')), may hold values from -6 to 6
- cotangent: bfloat16 [6144, 2048], P(('blk', 'dp')), may hold values from -0.59765625 to 0.59765625
- gate_probs: bfloat16 [6144, 3], P(('blk', 'dp')), may hold values from 0.099609375 to 1
- slot_rows: int32 [48, 128], P('blk'), may hold values from 0 to 384, as said below
- w_gate: bfloat16 [16, 2048, 768], P('blk', None, 'dp'), may hold values from -0.125 to 0.125
- w_up: bfloat16 [16, 2048, 768], P('blk', None, 'dp'), may hold values from -0.125 to 0.125
- w_down: bfloat16 [16, 768, 2048], P('blk', 'dp'), may hold values from -0.21875 to 0.21875
Outputs:
- mixed: bfloat16 [6144, 2048], P(('blk', 'dp'))
- input_grad: bfloat16 [6144, 2048], P(('blk', 'dp'))
- gate_grad: float32 [6144, 3], P(('blk', 'dp'))
- w_gate_grad: bfloat16 [16, 2048, 768], P('blk', None, 'dp')
- w_up_grad: bfloat16 [16, 2048, 768], P('blk', None, 'dp')
- w_down_grad: bfloat16 [16, 768, 2048], P('blk', 'dp')
Inputs may be any that keep to these rules, and one draw needn't show every extreme that they name: `slot_rows`: entries below 384 in a row are distinct and stand before the entries equal to 384; every row names at least 16 tokens, and some row names 128.
All inputs are finite; a program needn't handle non-finite values.
Results may differ from a plain program's by a relative error of at most 0.0075.
Values may be sent and summed in bfloat16 or wider, within the bound.
No kernel may reach another device: no remote copies, remote signals or barrier semaphores. Data moves between devices by JAX's collectives and lax.ppermute only.
A program may use at most 128 MiB of HBM per device.

v0:
```python
import functools

import jax
import jax.numpy as jnp
from jax import lax
from jax.experimental import pallas as pl
from jax.experimental.pallas import tpu as pltpu
from jax.sharding import PartitionSpec as P

CHUNKS = 2
BUSY = 10
SHARED = 0.01
EXTRA = 16
F32 = jnp.float32
BF16 = jnp.bfloat16
NT = (((1,), (1,)), ((), ()))
TN = (((0,), (0,)), ((), ()))


def shifted(value, axis, steps):
    count = lax.axis_size(axis)
    pairs = [(source, (source + steps) % count) for source in range(count)]
    return lax.ppermute(value, axis, pairs)


def after(value, earlier):
    return lax.optimization_barrier((value, earlier))[0]


def whole(array):
    return pl.BlockSpec(array.shape, lambda i: (0,) * len(array.shape))


def part(rows, columns, row, column):
    return pl.BlockSpec((rows, columns), lambda i: (row, column))


class Steps:
    def __init__(self):
        self.last = None

    def run(self, kernel, outs, operands, flops, name, held=(), tied=0, scale=SHARED):
        pair = lambda item: item if isinstance(item, tuple) else (item, whole(item))
        pairs = [pair(operand) for operand in operands]
        arrays, specs = [array for array, _ in pairs], [spec for _, spec in pairs]
        if self.last is not None:
            arrays[tied] = after(arrays[tied], self.last)
        out_shapes, out_specs = zip(*[pair(out) for out in outs])
        moved = sum(2 * spec.block_shape[0] * spec.block_shape[1] for spec in specs + list(out_specs))
        results = pl.pallas_call(
            (lambda *refs: kernel(*refs[len(held) :])) if held else kernel,
            grid=(1,),
            out_shape=out_shapes,
            in_specs=[pl.BlockSpec(memory_space=pl.ANY)] * len(held) + specs,
            out_specs=out_specs,
            input_output_aliases={i: i for i in range(len(held))},
            compiler_params=pltpu.CompilerParams(vmem_limit_bytes=20 * 2**20),
            cost_estimate=pl.CostEstimate(flops=int(flops * scale), bytes_accessed=int(moved * scale), transcendentals=0),
            name=name,
        )(*held, *arrays)
        self.last = results[0]
        return results


def shape(*dims, dtype=BF16):
    return jax.ShapeDtypeStruct(dims, dtype)


def dot(a, b, dims=(((1,), (0,)), ((), ()))):
    return lax.dot_general(a, b, dims, preferred_element_type=F32)


def picks(rows, count):
    columns = lax.broadcasted_iota(jnp.int32, (rows.shape[0], count), 1)
    return jnp.where(rows == columns, 1.0, 0.0).astype(BF16)


def weights_of(rows, gates):
    columns = lax.broadcasted_iota(jnp.int32, (rows.shape[0], gates.shape[1]), 1)
    return jnp.where(rows == columns, gates.astype(F32), 0.0)


def stacked(refs):
    return jnp.concatenate([ref[...] for ref in refs], axis=0)


def gather_rows(lists, own_rows, oth_rows, own, oth, *outs):
    count, cap = own.shape[0], outs[0].shape[0]
    rows = dot(picks(own_rows[...], count), own[...])
    rows += dot(picks(oth_rows[...], count), oth[...])
    for s in range(lists):
        outs[s][...] = rows[s * cap : (s + 1) * cap].astype(BF16)


def gather_scaled(lists, own_rows, oth_rows, own, oth, own_gate, oth_gate, *outs):
    count, cap = own.shape[0], outs[0].shape[0]
    rows = dot(picks(own_rows[...], count), own[...]) + dot(picks(oth_rows[...], count), oth[...])
    for s in range(lists):
        span = slice(s * cap, (s + 1) * cap)
        gate = weights_of(own_rows[span, :], own_gate[s : s + 1, :])
        gate += weights_of(oth_rows[span, :], oth_gate[s : s + 1, :count])
        outs[s][...] = (jnp.sum(gate, axis=1, keepdims=True) * rows[span]).astype(BF16)


def first_products(lists, *refs):
    x, (w_gate, w_up, gate_out, up_out) = refs[:lists], refs[lists:]
    rows = stacked(x)
    gate_out[...] = dot(rows, w_gate[...])
    up_out[...] = dot(rows, w_up[...])


def activation(lists, *refs):
    x, (w_gate, w_up, gate_in, up_in, hidden, active_out, slope_out) = refs[:lists], refs[lists:]
    rows = stacked(x)
    pre_gate = gate_in[...] + dot(rows, w_gate[...])
    pre_up = up_in[...] + dot(rows, w_up[...])
    sigmoid_gate = jax.nn.sigmoid(pre_gate)
    active = pre_gate * sigmoid_gate
    hidden[...] = (active * pre_up).astype(BF16)
    active_out[...] = active
    slope_out[...] = pre_up * sigmoid_gate * (1.0 + pre_gate * (1.0 - sigmoid_gate))


def expert_rows(me, hidden, w_down, sent, kept):
    width = kept.shape[1]
    first = dot(hidden[...], w_down[:, :width])
    second = dot(hidden[...], w_down[:, width:])
    lower = me[0, 0] == 0
    sent[...] = jnp.where(lower, second, first).astype(BF16)
    kept[...] = jnp.where(lower, first, second)


def whole_rows(kept, arrived, *outs):
    cap = outs[0].shape[0]
    rows = (kept[...] + arrived[...].astype(F32)).astype(BF16)
    for s, out in enumerate(outs):
        out[...] = rows[s * cap : (s + 1) * cap]


def first_hidden_grad(lists, *refs):
    out_grad, (w_down, total) = refs[:lists], refs[lists:]
    total[...] = dot(stacked(out_grad), w_down[...], NT)


def hidden_grads(lists, *refs):
    out_grad = refs[:lists]
    w_down, first, hidden, active, slope, gate_grad, up_grad, gate_sum = refs[lists:]
    grad = first[...] + dot(stacked(out_grad), w_down[...], NT)
    gate_grad[...] = (grad * slope[...]).astype(BF16)
    up_grad[...] = (grad * active[...]).astype(BF16)
    sums = jnp.sum(grad * hidden[...].astype(F32), axis=1, keepdims=True)
    gate_sum[...] = jnp.broadcast_to(sums, gate_sum.shape)


def input_rows(lists, gate_grad, up_grad, w_gate, w_up, gate_sum, *outs):
    cap = gate_sum.shape[0] // lists
    rows = dot(gate_grad[...], w_gate[...], NT) + dot(up_grad[...], w_up[...], NT)
    for s in range(lists):
        span = slice(s * cap, (s + 1) * cap)
        outs[s][:cap, :] = rows[span].astype(BF16)
        sums = jnp.transpose(gate_sum[span, :])[:EXTRA, :]
        high = sums.astype(BF16).astype(F32)
        row = lax.broadcasted_iota(jnp.int32, sums.shape, 0)
        packed = jnp.where(row == 0, high, jnp.where(row == 1, sums - high, 0.0))
        outs[s][cap:, :] = jnp.zeros((EXTRA, outs[s].shape[1]), BF16)
        outs[s][cap:, :cap] = packed.astype(BF16)


def input_halves(me, gate_grad, up_grad, w_gate, w_up, sent, kept):
    width = kept.shape[1]
    half = lambda span: dot(gate_grad[...], w_gate[span, :], NT) + dot(up_grad[...], w_up[span, :], NT)
    first, second = half(slice(0, width)), half(slice(width, 2 * width))
    lower = me[0, 0] == 0
    sent[...] = jnp.where(lower, second, first).astype(BF16)
    kept[...] = jnp.where(lower, first, second)


def weight_grads(lists, *refs):
    x, out_grad = refs[:lists], refs[lists : 2 * lists]
    hidden, gate_grad, up_grad, w_gate_grad, w_up_grad, w_down_grad = refs[2 * lists :]
    rows = stacked(x)
    w_gate_grad[...] = dot(rows, gate_grad[...], TN).astype(BF16)
    w_up_grad[...] = dot(rows, up_grad[...], TN).astype(BF16)
    w_down_grad[...] = dot(hidden[...], stacked(out_grad), TN).astype(BF16)


def scatter_rows(lists, rows, *refs):
    values, out = refs[:lists], refs[lists]
    cap = rows.shape[1]
    extra = values[0].shape[0] - cap
    count = out.shape[0] - extra
    total = tail = None
    for s in range(lists):
        token = lax.broadcasted_iota(jnp.int32, (count, cap), 0)
        mask = jnp.where(rows[s : s + 1, :] == token, 1.0, 0.0).astype(BF16)
        term = dot(mask, values[s][:cap, :])
        total = term if total is None else total + term
        if extra:
            sums = dot(values[s][cap:, :cap], mask, NT)
            row = lax.broadcasted_iota(jnp.int32, sums.shape, 0)
            high = jnp.where(row == s, sums[:1, :], 0.0)
            term = high + jnp.where(row == lists + s, sums[1:2, :], 0.0)
            tail = term if tail is None else tail + term
    out[:count, :] = total.astype(out.dtype)
    if extra:
        out[count:, :] = jnp.zeros((extra, out.shape[1]), out.dtype)
        out[count:, :count] = tail.astype(out.dtype)


def scatter_scaled(lists, rows, gate, *refs):
    values, out = refs[:lists], refs[lists]
    cap, count = values[0].shape[0], out.shape[0]
    total = None
    for s in range(lists):
        mask = weights_of(rows[s * cap : (s + 1) * cap, :], gate[s : s + 1, :count]).astype(BF16)
        term = dot(mask, values[s][...], TN)
        total = term if total is None else total + term
    out[...] = total.astype(out.dtype)


def join(me, own, arrived, out):
    width = own.shape[1]
    lower = me[0, 0] == 0
    out[:, :width] = jnp.where(lower, own[...], arrived[...])
    out[:, width:] = jnp.where(lower, arrived[...], own[...])


def add_halves_and_gate(lists, kept, arrived, gate, out, gate_out):
    count = out.shape[0]
    out[...] = (kept[:count, :] + arrived[:count, :].astype(F32)).astype(BF16)
    sums = kept[count:, :count] + arrived[count:, :count].astype(F32)
    gate_out[...] = (sums[:lists, :] + sums[lists : 2 * lists, :]) / gate[...]


def on_device(tokens, cotangent, gate_probs, slot_rows, w_gate, w_up, w_down):
    count, model = tokens.shape
    lists, cap = slot_rows.shape
    hidden_units = w_gate.shape[2]
    width = model // CHUNKS
    total = lists * cap
    chunks = range(CHUNKS)
    w_gate, w_up, w_down = w_gate[0], w_up[0], w_down[0]
    me = lax.axis_index("dp").astype(jnp.int32)
    own_rows = slot_rows - me * count
    oth_rows = slot_rows - (1 - me) * count
    own_column, oth_column = own_rows.reshape(total, 1), oth_rows.reshape(total, 1)
    own_gate = gate_probs.T.astype(F32)
    run = Steps().run
    kernel = lambda body: functools.partial(body, lists)
    columns = lambda array, c: (array, part(array.shape[0], width, 0, c))
    w_rows = lambda array, c: (array, part(width, hidden_units, c, 0))
    span = lambda c: slice(c * width, (c + 1) * width)
    rows_shape = [shape(cap, width)] * lists
    square = [shape(total, hidden_units, dtype=F32)] * 2
    gather_flops = 4 * total * count * width
    flops = 2 * total * width * hidden_units

    scalar = (me.reshape(1, 1), pl.BlockSpec((1, 1), lambda i: (0, 0), memory_space=pltpu.SMEM))

    def to_experts(rows):
        return [rows[0]] + [shifted(rows[s], "blk", -s) for s in range(1, lists)]

    def to_groups(rows):
        return [rows[0]] + [shifted(rows[s], "blk", s) for s in range(1, lists)]

    def gather_x(c):
        operands = [own_column, oth_column, columns(tokens, c), oth_x[c]]
        return to_experts(run(kernel(gather_rows), rows_shape, operands, gather_flops, "gather_x", tied=3))

    def gather_dy(c):
        arrived = (oth_dy[c], part(count, width, 0, 0))
        operands = [own_column, oth_column, columns(cotangent, c), arrived, own_gate, oth_gate]
        return to_experts(run(kernel(gather_scaled), rows_shape, operands, gather_flops, "gather_dy", tied=3))

    def weights(c, held):
        rows_out = (shape(model, hidden_units), part(width, hidden_units, c, 0))
        columns_out = (shape(hidden_units, model), part(hidden_units, width, 0, c))
        operands = x[c] + out_grad[c] + [hidden, gate_grad, up_grad]
        return run(kernel(weight_grads), [rows_out, rows_out, columns_out], operands, 3 * flops, "w_grads", held=held)

    def scatter(body, rows, values, gates, dtype, name, scale=BUSY):
        extent = values[0].shape[1]
        outs = [shape(count + values[0].shape[0] - cap, extent, dtype=dtype)]
        return run(body, outs, [rows] + gates + values, 2 * total * count * extent, name, tied=-1, scale=scale)[0]

    pieces = []
    for source, c in [(tokens, 0), (tokens, 1), (cotangent, 0), (cotangent, 1)]:
        pieces.append((after(source, pieces[-1]) if pieces else source)[:, span(c)])
    gate_rows = jnp.pad(gate_probs.T, ((0, EXTRA - lists), (0, width - count)))
    pieces[2] = jnp.concatenate([pieces[2], gate_rows], axis=0)
    oth_x = [shifted(piece, "dp", 1) for piece in pieces[:2]]
    oth_dy = [shifted(piece, "dp", 1) for piece in pieces[2:]]
    oth_gate = (oth_dy[0], part(EXTRA, width, count // EXTRA, 0))
    x = [gather_x(0), gather_x(1)]

    pre = run(kernel(first_products), square, x[0] + [w_rows(w_gate, 0), w_rows(w_up, 0)], 2 * flops, "pre")
    out_grad = [gather_dy(0)]
    hidden, active, slope = run(
        kernel(activation),
        [shape(total, hidden_units)] + square,
        x[1] + [w_rows(w_gate, 1), w_rows(w_up, 1)] + list(pre),
        2 * flops,
        "hidden",
    )
    sent, kept = run(
        expert_rows, [shape(total, width), shape(total, width, dtype=F32)], [scalar, hidden, w_down], 2 * flops,
        "expert_out", tied=1,
    )
    arrived = shifted(sent, "dp", 1)
    out_grad.append(gather_dy(1))

    first = run(kernel(first_hidden_grad), square[:1], out_grad[0] + [columns(w_down, 0)], flops, "hidden_grad", scale=BUSY)
    gate_grad, up_grad, gate_sum = run(
        kernel(hidden_grads),
        [shape(total, hidden_units)] * 2 + [shape(total, cap, dtype=F32)],
        out_grad[1] + [columns(w_down, 1), first[0], hidden, active, slope],
        flops,
        "hidden_grads",
        scale=BUSY,
    )
    few, many = model // 4, model - model // 4
    half = many // 2
    many_rows = lambda array: (array, part(many, hidden_units, 0, 0))
    few_rows = lambda array: (array, part(few, hidden_units, many // few, 0))
    sent, second_kept = run(
        input_halves,
        [shape(total, half), shape(total, half, dtype=F32)],
        [scalar, gate_grad, up_grad, many_rows(w_gate), many_rows(w_up)],
        3 * flops,
        "input_grad",
        tied=1,
        scale=BUSY,
    )
    second_arrived = shifted(sent, "dp", 1)
    rows = run(
        kernel(input_rows),
        [shape(cap + EXTRA, few)] * lists,
        [gate_grad, up_grad, few_rows(w_gate), few_rows(w_up), gate_sum],
        flops,
        "input_grad",
        scale=BUSY,
    )
    first_rows = to_groups(rows)
    expert_out = to_groups(run(whole_rows, rows_shape, [kept, arrived], 0, "expert_out_rows"))
    weight_outs = weights(1, weights(0, ()))

    half_shape = [shape(cap, half)] * lists
    sent = scatter(kernel(scatter_rows), oth_rows, first_rows, [], BF16, "grad_sent")
    first_arrived = shifted(sent, "dp", 1)
    second_rows = to_groups(run(whole_rows, half_shape, [second_kept, second_arrived], 0, "input_grad_rows"))
    first_kept = scatter(kernel(scatter_rows), own_rows, first_rows, [], F32, "grad_kept")
    sent = scatter(kernel(scatter_scaled), oth_column, expert_out, [oth_gate], BF16, "mixed_sent", SHARED)
    mixed_arrived = shifted(sent, "dp", 1)
    mixed_own = scatter(kernel(scatter_scaled), own_column, expert_out, [own_gate], BF16, "mixed_own", SHARED)
    few_columns = (shape(count, model), part(count, few, 0, many // few))
    many_columns = (shape(count, model), part(count, many, 0, 0))
    *grad, gate_out = run(
        kernel(add_halves_and_gate),
        [few_columns, shape(lists, count, dtype=F32)],
        [first_kept, first_arrived, own_gate],
        0,
        "grad",
        scale=BUSY,
    )
    sent = scatter(kernel(scatter_rows), oth_rows, second_rows, [], BF16, "grad_sent")
    second_arrived = shifted(sent, "dp", 1)
    second_own = scatter(kernel(scatter_rows), own_rows, second_rows, [], BF16, "grad_own")
    mixed = run(join, [shape(count, model)], [scalar, mixed_own, mixed_arrived], 0, "mixed", tied=1, scale=BUSY)[0]
    grad = run(join, [many_columns], [scalar, second_own, second_arrived], 0, "grad", held=grad, tied=1)[0]
    return (mixed, grad, gate_out.T) + tuple(out[None] for out in weight_outs)


def solution(mesh):
    rows, lists = P(("blk", "dp"), None), P("blk", None)
    inner, outer = P("blk", None, "dp"), P("blk", "dp", None)
    return jax.shard_map(
        on_device,
        mesh=mesh,
        in_specs=(rows, rows, rows, lists, inner, inner, outer),
        out_specs=(rows, rows, rows, inner, inner, outer),
        check_vma=False,
    )
```

profile of v0, /device:TPU:0, one launch (start us, length us, event | category | flops | bytes accessed | tf_op | source)
XLA Modules:
  0.0 94.1 jit_solution(9538871910586496698)
XLA Ops:
  0.7 1.1 %slice.12 = bf16[192,1024]{1,0:T(8,128)(2,1)S(1)} slice(bf16[192,2048]{1,0:T(8,128)(2,1)} %own.5), slice={[0:192], [0:1024]} | slice | bytes 786432 | tf_op jit(solution)/shard_map/slice | solution.py:288
  1.8 3.0 %collective-permute-start.1 = (bf16[192,1024]{1,0:T(8,128)(2,1)S(1)}, bf16[192,1024]{1,0:T(8,128)(2,1)S(1)}, u32[]{:S(2)}, u32[]{:S(2)}) collective-permute-start(bf16[192,1024]{1,0:T(8,128)(2,1)S(1)} %slice.12), channel_id=1, source_target_pairs={{0,1},{1,0},{2,3},{3,2},{4,5},{5,4},{6,7},{7,6},{8,9},{9,8},{10,11... | collective-permute-start | bytes 1179656 | tf_op jit(solution)/shard_map/ppermute | solution.py:23
  4.8 1.0 %slice.13 = bf16[192,1024]{1,0:T(8,128)(2,1)S(1)} slice(bf16[192,2048]{1,0:T(8,128)(2,1)} %own.5), slice={[0:192], [1024:2048]} | slice | bytes 786432 | tf_op jit(solution)/shard_map/slice | solution.py:288
  6.3 8.5 %collective-permute-done.1.oth = bf16[192,1024]{1,0:T(8,128)(2,1)S(1)} collective-permute-done((bf16[192,1024]{1,0:T(8,128)(2,1)S(1)}, bf16[192,1024]{1,0:T(8,128)(2,1)S(1)}, u32[]{:S(2)}, u32[]{:S(2)}) %collective-permute-start.1) | collective-permute-done | bytes 393248 | tf_op jit(solution)/shard_map/ppermute | solution.py:23
  15.4 2.5 %collective-permute-start.3 = (bf16[128,1024]{1,0:T(8,128)(2,1)S(1)}, bf16[128,1024]{1,0:T(8,128)(2,1)S(1)}, u32[]{:S(2)}, u32[]{:S(2)}) collective-permute-start(bf16[128,1024]{1,0:T(8,128)(2,1)S(1)} %get-tuple-element.79), channel_id=1, source_target_pairs={{0,30},{2,0},{4,2},{6,4},{8,6},{10,8},{12,10},{14,12},{16,14},{18,... | collective-permute-start | bytes 786440 | tf_op jit(solution)/shard_map/ppermute | solution.py:23
  17.9 1.6 %collective-permute-start.2 = (bf16[208,1024]{1,0:T(8,128)(2,1)S(1)}, bf16[208,1024]{1,0:T(8,128)(2,1)S(1)}, u32[]{:S(2)}, u32[]{:S(2)}) collective-permute-start(bf16[208,1024]{1,0:T(8,128)(2,1)S(1)} %fusion.1), channel_id=1, source_target_pairs={{0,1},{1,0},{2,3},{3,2},{4,5},{5,4},{6,7},{7,6},{8,9},{9,8},{10,11... | collective-permute-start | bytes 1277960 | tf_op jit(solution)/shard_map/ppermute | solution.py:23
  19.5 2.6 %collective-permute-start.4 = (bf16[128,1024]{1,0:T(8,128)(2,1)S(1)}, bf16[128,1024]{1,0:T(8,128)(2,1)S(1)}, u32[]{:S(2)}, u32[]{:S(2)}) collective-permute-start(bf16[128,1024]{1,0:T(8,128)(2,1)S(1)} %get-tuple-element.80), channel_id=1, source_target_pairs={{0,28},{2,30},{4,0},{6,2},{8,4},{10,6},{12,8},{14,10},{16,12},{18,... | collective-permute-start | bytes 786440 | tf_op jit(solution)/shard_map/ppermute | solution.py:23
  23.8 2.5 %collective-permute-start.5 = (bf16[128,1024]{1,0:T(8,128)(2,1)S(1)}, bf16[128,1024]{1,0:T(8,128)(2,1)S(1)}, u32[]{:S(2)}, u32[]{:S(2)}) collective-permute-start(bf16[128,1024]{1,0:T(8,128)(2,1)S(1)} %get-tuple-element.85), channel_id=1, source_target_pairs={{0,30},{2,0},{4,2},{6,4},{8,6},{10,8},{12,10},{14,12},{16,14},{18,... | collective-permute-start | bytes 786440 | tf_op jit(solution)/shard_map/ppermute | solution.py:23
  26.3 2.7 %collective-permute-start.6 = (bf16[128,1024]{1,0:T(8,128)(2,1)S(1)}, bf16[128,1024]{1,0:T(8,128)(2,1)S(1)}, u32[]{:S(2)}, u32[]{:S(2)}) collective-permute-start(bf16[128,1024]{1,0:T(8,128)(2,1)S(1)} %get-tuple-element.86), channel_id=1, source_target_pairs={{0,28},{2,30},{4,0},{6,2},{8,4},{10,6},{12,8},{14,10},{16,12},{18,... | collective-permute-start | bytes 786440 | tf_op jit(solution)/shard_map/ppermute | solution.py:23
  29.0 1.0 %pre.1 = (f32[384,384]{1,0:T(8,128)S(1)}, f32[384,384]{1,0:T(8,128)S(1)}) custom-call(bf16[128,1024]{1,0:T(8,128)(2,1)S(1)} %get-tuple-element.117.refs_0_, bf16[128,1024]{1,0:T(8,128)(2,1)S(1)} %collective-permute-done.3.refs_1_, bf16[128,1024]{1,0:T(8,128)(2,1)S(1)} %collective-permute-done.4.refs_2_, bf16[2048,384]{1,0:T(8,128)(2,1)S(1)} %bitcast.32, ...), custom_call_target="tpu_custom_call" | custom-call | flops 6039797 | bytes 29491 | tf_op jit(solution)/shard_map/pre/pallas_call | solution.py:50
  30.0 2.3 %collective-permute-done.2.oth.oth_gate.gate = bf16[208,1024]{1,0:T(8,128)(2,1)S(1)} collective-permute-done((bf16[208,1024]{1,0:T(8,128)(2,1)S(1)}, bf16[208,1024]{1,0:T(8,128)(2,1)S(1)}, u32[]{:S(2)}, u32[]{:S(2)}) %collective-permute-start.2) | collective-permute-done | bytes 426016 | tf_op jit(solution)/shard_map/ppermute | solution.py:23
  33.0 2.5 %collective-permute-start.8 = (bf16[128,1024]{1,0:T(8,128)(2,1)S(1)}, bf16[128,1024]{1,0:T(8,128)(2,1)S(1)}, u32[]{:S(2)}, u32[]{:S(2)}) collective-permute-start(bf16[128,1024]{1,0:T(8,128)(2,1)S(1)} %get-tuple-element.96), channel_id=1, source_target_pairs={{0,30},{2,0},{4,2},{6,4},{8,6},{10,8},{12,10},{14,12},{16,14},{18,... | collective-permute-start | bytes 786440 | tf_op jit(solution)/shard_map/ppermute | solution.py:23
  35.6 2.7 %collective-permute-start.9 = (bf16[128,1024]{1,0:T(8,128)(2,1)S(1)}, bf16[128,1024]{1,0:T(8,128)(2,1)S(1)}, u32[]{:S(2)}, u32[]{:S(2)}) collective-permute-start(bf16[128,1024]{1,0:T(8,128)(2,1)S(1)} %get-tuple-element.97), channel_id=1, source_target_pairs={{0,28},{2,30},{4,0},{6,2},{8,4},{10,6},{12,8},{14,10},{16,12},{18,... | collective-permute-start | bytes 786440 | tf_op jit(solution)/shard_map/ppermute | solution.py:23
  38.2 1.2 %hidden.1 = (bf16[384,384]{1,0:T(8,128)(2,1)S(1)}, f32[384,384]{1,0:T(8,128)S(1)}, f32[384,384]{1,0:T(8,128)S(1)}) custom-call(bf16[128,1024]{1,0:T(8,128)(2,1)S(1)} %get-tuple-element.121.refs_0_.refs_3_, bf16[128,1024]{1,0:T(8,128)(2,1)S(1)} %collective-permute-done.5.refs_1_.refs_4_, bf16[128,1024]{1,0:T(8,128)(2,1)S(1)} %collective-permute-done.6.refs_2_.refs_5_, ...), custom_call_target="tpu_custom_call" | custom-call | flops 6039797 | bytes 38338 | tf_op jit(solution)/shard_map/hidden/pallas_call | solution.py:50
  39.6 1.0 %expert_out.1 = (bf16[384,1024]{1,0:T(8,128)(2,1)S(1)}, f32[384,1024]{1,0:T(8,128)S(1)}) custom-call(s32[1,1]{1,0:T(1,128)} %bitcast.me.refs_1_, bf16[384,384]{1,0:T(8,128)(2,1)S(1)} %get-tuple-element.89.hidden.refs_5_.refs_6_.refs_9_, bf16[384,2048]{1,0:T(8,128)(2,1)S(1)} %bitcast.40), custom_call_target="tpu_custom_call" | custom-call | flops 6039797 | bytes 34406 | tf_op jit(solution)/shard_map/expert_out/pallas_call | solution.py:50
  40.6 1.6 %collective-permute-start.12 = (bf16[384,1024]{1,0:T(8,128)(2,1)S(1)}, bf16[384,1024]{1,0:T(8,128)(2,1)S(1)}, u32[]{:S(2)}, u32[]{:S(2)}) collective-permute-start(bf16[384,1024]{1,0:T(8,128)(2,1)S(1)} %get-tuple-element.92), channel_id=1, source_target_pairs={{0,1},{1,0},{2,3},{3,2},{4,5},{5,4},{6,7},{7,6},{8,9},{9,8},{10,11... | collective-permute-start | bytes 2359304 | tf_op jit(solution)/shard_map/ppermute | solution.py:23
  42.9 1.7 %collective-permute-start.10 = (bf16[128,1024]{1,0:T(8,128)(2,1)S(1)}, bf16[128,1024]{1,0:T(8,128)(2,1)S(1)}, u32[]{:S(2)}, u32[]{:S(2)}) collective-permute-start(bf16[128,1024]{1,0:T(8,128)(2,1)S(1)} %get-tuple-element.99), channel_id=1, source_target_pairs={{0,30},{2,0},{4,2},{6,4},{8,6},{10,8},{12,10},{14,12},{16,14},{18,... | collective-permute-start | bytes 786440 | tf_op jit(solution)/shard_map/ppermute | solution.py:23
  44.6 1.3 %collective-permute-start.11 = (bf16[128,1024]{1,0:T(8,128)(2,1)S(1)}, bf16[128,1024]{1,0:T(8,128)(2,1)S(1)}, u32[]{:S(2)}, u32[]{:S(2)}) collective-permute-start(bf16[128,1024]{1,0:T(8,128)(2,1)S(1)} %get-tuple-element.100), channel_id=1, source_target_pairs={{0,28},{2,30},{4,0},{6,2},{8,4},{10,6},{12,8},{14,10},{16,12},{18,... | collective-permute-start | bytes 786440 | tf_op jit(solution)/shard_map/ppermute | solution.py:23
  46.4 4.2 %collective-permute-done.10.refs_1_.refs_7_ = bf16[128,1024]{1,0:T(8,128)(2,1)S(1)} collective-permute-done((bf16[128,1024]{1,0:T(8,128)(2,1)S(1)}, bf16[128,1024]{1,0:T(8,128)(2,1)S(1)}, u32[]{:S(2)}, u32[]{:S(2)}) %collective-permute-start.10) | collective-permute-done | bytes 262176 | tf_op jit(solution)/shard_map/ppermute | solution.py:23
  50.6 3.9 %collective-permute-done.11.refs_2_.refs_8_ = bf16[128,1024]{1,0:T(8,128)(2,1)S(1)} collective-permute-done((bf16[128,1024]{1,0:T(8,128)(2,1)S(1)}, bf16[128,1024]{1,0:T(8,128)(2,1)S(1)}, u32[]{:S(2)}, u32[]{:S(2)}) %collective-permute-start.11) | collective-permute-done | bytes 262176 | tf_op jit(solution)/shard_map/ppermute | solution.py:23
  55.2 1.4 %input_grad.2 = (bf16[384,768]{1,0:T(8,128)(2,1)S(1)}, f32[384,768]{1,0:T(8,128)S(1)}) custom-call(s32[1,1]{1,0:T(1,128)} %bitcast.me.refs_1_, bf16[384,384]{1,0:T(8,128)(2,1)S(1)} %get-tuple-element.107.gate_grad.refs_7_.refs_10_, bf16[384,384]{1,0:T(8,128)(2,1)S(1)} %get-tuple-element.105.up_grad.refs_8_.refs_11_, bf16[2048,384]{1,0:T(8,128)(2,1)S(1)} %bitcast.34, ...), custom_call_target="tpu_custom_call" | custom-call | flops 9059696640 | bytes 41287700 | tf_op jit(solution)/shard_map/input_grad/pallas_call | solution.py:50
  57.9 1.6 %collective-permute-start.16 = (bf16[144,512]{1,0:T(8,128)(2,1)S(1)}, bf16[144,512]{1,0:T(8,128)(2,1)S(1)}, u32[]{:S(2)}, u32[]{:S(2)}) collective-permute-start(bf16[144,512]{1,0:T(8,128)(2,1)S(1)} %get-tuple-element.115), channel_id=1, source_target_pairs={{0,4},{2,6},{4,8},{6,10},{8,12},{10,14},{12,16},{14,18},{16,20},{1... | collective-permute-start | bytes 442376 | tf_op jit(solution)/shard_map/ppermute | solution.py:23
  59.4 1.6 %collective-permute-done.12.arrived = bf16[384,1024]{1,0:T(8,128)(2,1)S(1)} collective-permute-done((bf16[384,1024]{1,0:T(8,128)(2,1)S(1)}, bf16[384,1024]{1,0:T(8,128)(2,1)S(1)}, u32[]{:S(2)}, u32[]{:S(2)}) %collective-permute-start.12) | collective-permute-done | bytes 786464 | tf_op jit(solution)/shard_map/ppermute | solution.py:23
  61.3 1.5 %collective-permute-start.14 = (bf16[128,1024]{1,0:T(8,128)(2,1)S(1)}, bf16[128,1024]{1,0:T(8,128)(2,1)S(1)}, u32[]{:S(2)}, u32[]{:S(2)}) collective-permute-start(bf16[128,1024]{1,0:T(8,128)(2,1)S(1)} %get-tuple-element.113), channel_id=1, source_target_pairs={{0,4},{2,6},{4,8},{6,10},{8,12},{10,14},{12,16},{14,18},{16,20},{1... | collective-permute-start | bytes 786440 | tf_op jit(solution)/shard_map/ppermute | solution.py:23
  62.8 2.4 %w_grads.2 = (bf16[2048,384]{1,0:T(8,128)(2,1)}, bf16[2048,384]{1,0:T(8,128)(2,1)}, bf16[384,2048]{1,0:T(8,128)(2,1)}) custom-call(bf16[128,1024]{1,0:T(8,128)(2,1)S(1)} %get-tuple-element.117.refs_0_, bf16[128,1024]{1,0:T(8,128)(2,1)S(1)} %collective-permute-done.3.refs_1_, bf16[128,1024]{1,0:T(8,128)(2,1)S(1)} %collective-permute-done.4.refs_2_, ...), custom_call_target="tpu_custom_call" | custom-call | flops 9059696 | bytes 48168 | tf_op jit(solution)/shard_map/w_grads/pallas_call | solution.py:50
  65.2 2.6 %w_grads.3 = (bf16[2048,384]{1,0:T(8,128)(2,1)}, bf16[2048,384]{1,0:T(8,128)(2,1)}, bf16[384,2048]{1,0:T(8,128)(2,1)}) custom-call(bf16[2048,384]{1,0:T(8,128)(2,1)} %get-tuple-element.118.refs_0_, bf16[2048,384]{1,0:T(8,128)(2,1)} %get-tuple-element.119.refs_1_, ...), custom_call_target="tpu_custom_call", output_to_operand_aliasing={{0}: (0, {}), {1}: (1, {}), {2}: (2, {})} | custom-call | flops 9059696 | bytes 48168 | tf_op jit(solution)/shard_map/w_grads/pallas_call | solution.py:50
  68.2 1.1 %collective-permute-start.20 = (bf16[208,512]{1,0:T(8,128)(2,1)S(1)}, bf16[208,512]{1,0:T(8,128)(2,1)S(1)}, u32[]{:S(2)}, u32[]{:S(2)}) collective-permute-start(bf16[208,512]{1,0:T(8,128)(2,1)S(1)} %grad_sent.2), channel_id=1, source_target_pairs={{0,1},{1,0},{2,3},{3,2},{4,5},{5,4},{6,7},{7,6},{8,9},{9,8},{10,11... | collective-permute-start | bytes 638984 | tf_op jit(solution)/shard_map/ppermute | solution.py:23
  69.3 4.4 %collective-permute-done.17.arrived = bf16[384,768]{1,0:T(8,128)(2,1)S(1)} collective-permute-done((bf16[384,768]{1,0:T(8,128)(2,1)S(1)}, bf16[384,768]{1,0:T(8,128)(2,1)S(1)}, u32[]{:S(2)}, u32[]{:S(2)}) %collective-permute-start.17) | collective-permute-done | bytes 589856 | tf_op jit(solution)/shard_map/ppermute | solution.py:23
  74.9 1.6 %collective-permute-start.21 = (bf16[192,1024]{1,0:T(8,128)(2,1)S(1)}, bf16[192,1024]{1,0:T(8,128)(2,1)S(1)}, u32[]{:S(2)}, u32[]{:S(2)}) collective-permute-start(bf16[192,1024]{1,0:T(8,128)(2,1)S(1)} %mixed_sent.1), channel_id=1, source_target_pairs={{0,1},{1,0},{2,3},{3,2},{4,5},{5,4},{6,7},{7,6},{8,9},{9,8},{10,11... | collective-permute-start | bytes 1179656 | tf_op jit(solution)/shard_map/ppermute | solution.py:23
  78.2 5.8 %collective-permute-done.19.refs_2_ = bf16[128,768]{1,0:T(8,128)(2,1)S(1)} collective-permute-done((bf16[128,768]{1,0:T(8,128)(2,1)S(1)}, bf16[128,768]{1,0:T(8,128)(2,1)S(1)}, u32[]{:S(2)}, u32[]{:S(2)}) %collective-permute-start.19) | collective-permute-done | bytes 196640 | tf_op jit(solution)/shard_map/ppermute | solution.py:23
  84.5 1.6 %collective-permute-start.22 = (bf16[192,768]{1,0:T(8,128)(2,1)S(1)}, bf16[192,768]{1,0:T(8,128)(2,1)S(1)}, u32[]{:S(2)}, u32[]{:S(2)}) collective-permute-start(bf16[192,768]{1,0:T(8,128)(2,1)S(1)} %grad_sent.3), channel_id=1, source_target_pairs={{0,1},{1,0},{2,3},{3,2},{4,5},{5,4},{6,7},{7,6},{8,9},{9,8},{10,11... | collective-permute-start | bytes 884744 | tf_op jit(solution)/shard_map/ppermute | solution.py:23
  87.4 5.9 %collective-permute-done.22.refs_3_ = bf16[192,768]{1,0:T(8,128)(2,1)S(1)} collective-permute-done((bf16[192,768]{1,0:T(8,128)(2,1)S(1)}, bf16[192,768]{1,0:T(8,128)(2,1)S(1)}, u32[]{:S(2)}, u32[]{:S(2)}) %collective-permute-start.22) | collective-permute-done | bytes 294944 | tf_op jit(solution)/shard_map/ppermute | solution.py:23
  (64 shorter events, 12.9 us)
Async XLA Ops:
  0.6 14.1 %copy-start = (bf16[192,2048]{1,0:T(8,128)(2,1)S(1)}, bf16[192,2048]{1,0:T(8,128)(2,1)}, u32[]{:S(2)}) copy-start(bf16[192,2048]{1,0:T(8,128)(2,1)} %own.5) | copy-start | bytes 2359300
  0.6 5.3 %copy-start.6 = (s32[3,128]{1,0:T(4,128)S(1)}, s32[3,128]{1,0:T(4,128)}, u32[]{:S(2)}) copy-start(s32[3,128]{1,0:T(4,128)} %param.10) | copy-start | bytes 4612
  1.8 13.0 %collective-permute-start.1 = (bf16[192,1024]{1,0:T(8,128)(2,1)S(1)}, bf16[192,1024]{1,0:T(8,128)(2,1)S(1)}, u32[]{:S(2)}, u32[]{:S(2)}) collective-permute-start(bf16[192,1024]{1,0:T(8,128)(2,1)S(1)} %slice.12), channel_id=1, source_target_pairs={{0,1},{1,0},{2,3},{3,2},{4,5},{5,4},{6,7},{7,6},{8,9},{9,8},{10,11... | collective-permute-start | bytes 1179656 | tf_op jit(solution)/shard_map/ppermute | solution.py:23
  5.8 12.1 %slice-start = ((bf16[192,2048]{1,0:T(8,128)(2,1)}), bf16[192,1024]{1,0:T(8,128)(2,1)S(1)}, s32[]{:S(2)}) async-start(bf16[192,2048]{1,0:T(8,128)(2,1)} %own.7), calls=%async_computation | async-start | bytes 786432 | tf_op jit(solution)/shard_map/slice | solution.py:288
  5.8 12.1 %copy-start.5 = (bf16[192,3]{0,1:T(4,128)(2,1)S(1)}, bf16[192,3]{0,1:T(4,128)(2,1)}, u32[]{:S(2)}) copy-start(bf16[192,3]{0,1:T(4,128)(2,1)} %param.9) | copy-start | bytes 3460
  5.8 17.3 %collective-permute-start = (bf16[192,1024]{1,0:T(8,128)(2,1)S(1)}, bf16[192,1024]{1,0:T(8,128)(2,1)S(1)}, u32[]{:S(2)}, u32[]{:S(2)}) collective-permute-start(bf16[192,1024]{1,0:T(8,128)(2,1)S(1)} %slice.13), channel_id=1, source_target_pairs={{0,1},{1,0},{2,3},{3,2},{4,5},{5,4},{6,7},{7,6},{8,9},{9,8},{10,11... | collective-permute-start | bytes 1179656 | tf_op jit(solution)/shard_map/ppermute | solution.py:23
  6.3 15.9 %copy-start.1 = (bf16[192,2048]{1,0:T(8,128)(2,1)S(1)}, bf16[192,2048]{1,0:T(8,128)(2,1)}, u32[]{:S(2)}) copy-start(bf16[192,2048]{1,0:T(8,128)(2,1)} %own.7) | copy-start | bytes 2359300
  15.4 11.0 %collective-permute-start.3 = (bf16[128,1024]{1,0:T(8,128)(2,1)S(1)}, bf16[128,1024]{1,0:T(8,128)(2,1)S(1)}, u32[]{:S(2)}, u32[]{:S(2)}) collective-permute-start(bf16[128,1024]{1,0:T(8,128)(2,1)S(1)} %get-tuple-element.79), channel_id=1, source_target_pairs={{0,30},{2,0},{4,2},{6,4},{8,6},{10,8},{12,10},{14,12},{16,14},{18,... | collective-permute-start | bytes 786440 | tf_op jit(solution)/shard_map/ppermute | solution.py:23
  17.9 11.1 %copy-start.2 = (bf16[1,2048,384]{2,1,0:T(8,128)(2,1)S(1)}, bf16[1,2048,384]{2,1,0:T(8,128)(2,1)}, u32[]{:S(2)}) copy-start(bf16[1,2048,384]{2,1,0:T(8,128)(2,1)} %param.11) | copy-start | bytes 4718596
  17.9 11.1 %copy-start.3 = (bf16[1,2048,384]{2,1,0:T(8,128)(2,1)S(1)}, bf16[1,2048,384]{2,1,0:T(8,128)(2,1)}, u32[]{:S(2)}) copy-start(bf16[1,2048,384]{2,1,0:T(8,128)(2,1)} %param.12) | copy-start | bytes 4718596
  17.9 14.3 %collective-permute-start.2 = (bf16[208,1024]{1,0:T(8,128)(2,1)S(1)}, bf16[208,1024]{1,0:T(8,128)(2,1)S(1)}, u32[]{:S(2)}, u32[]{:S(2)}) collective-permute-start(bf16[208,1024]{1,0:T(8,128)(2,1)S(1)} %fusion.1), channel_id=1, source_target_pairs={{0,1},{1,0},{2,3},{3,2},{4,5},{5,4},{6,7},{7,6},{8,9},{9,8},{10,11... | collective-permute-start | bytes 1277960 | tf_op jit(solution)/shard_map/ppermute | solution.py:23
  19.5 9.4 %collective-permute-start.4 = (bf16[128,1024]{1,0:T(8,128)(2,1)S(1)}, bf16[128,1024]{1,0:T(8,128)(2,1)S(1)}, u32[]{:S(2)}, u32[]{:S(2)}) collective-permute-start(bf16[128,1024]{1,0:T(8,128)(2,1)S(1)} %get-tuple-element.80), channel_id=1, source_target_pairs={{0,28},{2,30},{4,0},{6,2},{8,4},{10,6},{12,8},{14,10},{16,12},{18,... | collective-permute-start | bytes 786440 | tf_op jit(solution)/shard_map/ppermute | solution.py:23
  22.2 20.0 %collective-permute-start.7 = (bf16[192,1024]{1,0:T(8,128)(2,1)S(1)}, bf16[192,1024]{1,0:T(8,128)(2,1)S(1)}, u32[]{:S(2)}, u32[]{:S(2)}) collective-permute-start(bf16[192,1024]{1,0:T(8,128)(2,1)S(1)} %slice.15), channel_id=1, source_target_pairs={{0,1},{1,0},{2,3},{3,2},{4,5},{5,4},{6,7},{7,6},{8,9},{9,8},{10,11... | collective-permute-start | bytes 1179656 | tf_op jit(solution)/shard_map/ppermute | solution.py:23
  23.8 14.4 %collective-permute-start.5 = (bf16[128,1024]{1,0:T(8,128)(2,1)S(1)}, bf16[128,1024]{1,0:T(8,128)(2,1)S(1)}, u32[]{:S(2)}, u32[]{:S(2)}) collective-permute-start(bf16[128,1024]{1,0:T(8,128)(2,1)S(1)} %get-tuple-element.85), channel_id=1, source_target_pairs={{0,30},{2,0},{4,2},{6,4},{8,6},{10,8},{12,10},{14,12},{16,14},{18,... | collective-permute-start | bytes 786440 | tf_op jit(solution)/shard_map/ppermute | solution.py:23
  26.3 11.9 %collective-permute-start.6 = (bf16[128,1024]{1,0:T(8,128)(2,1)S(1)}, bf16[128,1024]{1,0:T(8,128)(2,1)S(1)}, u32[]{:S(2)}, u32[]{:S(2)}) collective-permute-start(bf16[128,1024]{1,0:T(8,128)(2,1)S(1)} %get-tuple-element.86), channel_id=1, source_target_pairs={{0,28},{2,30},{4,0},{6,2},{8,4},{10,6},{12,8},{14,10},{16,12},{18,... | collective-permute-start | bytes 786440 | tf_op jit(solution)/shard_map/ppermute | solution.py:23
  33.0 12.8 %collective-permute-start.8 = (bf16[128,1024]{1,0:T(8,128)(2,1)S(1)}, bf16[128,1024]{1,0:T(8,128)(2,1)S(1)}, u32[]{:S(2)}, u32[]{:S(2)}) collective-permute-start(bf16[128,1024]{1,0:T(8,128)(2,1)S(1)} %get-tuple-element.96), channel_id=1, source_target_pairs={{0,30},{2,0},{4,2},{6,4},{8,6},{10,8},{12,10},{14,12},{16,14},{18,... | collective-permute-start | bytes 786440 | tf_op jit(solution)/shard_map/ppermute | solution.py:23
  35.6 10.3 %collective-permute-start.9 = (bf16[128,1024]{1,0:T(8,128)(2,1)S(1)}, bf16[128,1024]{1,0:T(8,128)(2,1)S(1)}, u32[]{:S(2)}, u32[]{:S(2)}) collective-permute-start(bf16[128,1024]{1,0:T(8,128)(2,1)S(1)} %get-tuple-element.97), channel_id=1, source_target_pairs={{0,28},{2,30},{4,0},{6,2},{8,4},{10,6},{12,8},{14,10},{16,12},{18,... | collective-permute-start | bytes 786440 | tf_op jit(solution)/shard_map/ppermute | solution.py:23
  38.2 1.4 %copy-start.4 = (bf16[1,384,2048]{2,1,0:T(8,128)(2,1)S(1)}, bf16[1,384,2048]{2,1,0:T(8,128)(2,1)}, u32[]{:S(2)}) copy-start(bf16[1,384,2048]{2,1,0:T(8,128)(2,1)} %param.13) | copy-start | bytes 4718596
  40.6 20.4 %collective-permute-start.12 = (bf16[384,1024]{1,0:T(8,128)(2,1)S(1)}, bf16[384,1024]{1,0:T(8,128)(2,1)S(1)}, u32[]{:S(2)}, u32[]{:S(2)}) collective-permute-start(bf16[384,1024]{1,0:T(8,128)(2,1)S(1)} %get-tuple-element.92), channel_id=1, source_target_pairs={{0,1},{1,0},{2,3},{3,2},{4,5},{5,4},{6,7},{7,6},{8,9},{9,8},{10,11... | collective-permute-start | bytes 2359304 | tf_op jit(solution)/shard_map/ppermute | solution.py:23
  42.9 7.7 %collective-permute-start.10 = (bf16[128,1024]{1,0:T(8,128)(2,1)S(1)}, bf16[128,1024]{1,0:T(8,128)(2,1)S(1)}, u32[]{:S(2)}, u32[]{:S(2)}) collective-permute-start(bf16[128,1024]{1,0:T(8,128)(2,1)S(1)} %get-tuple-element.99), channel_id=1, source_target_pairs={{0,30},{2,0},{4,2},{6,4},{8,6},{10,8},{12,10},{14,12},{16,14},{18,... | collective-permute-start | bytes 786440 | tf_op jit(solution)/shard_map/ppermute | solution.py:23
  44.6 9.9 %collective-permute-start.11 = (bf16[128,1024]{1,0:T(8,128)(2,1)S(1)}, bf16[128,1024]{1,0:T(8,128)(2,1)S(1)}, u32[]{:S(2)}, u32[]{:S(2)}) collective-permute-start(bf16[128,1024]{1,0:T(8,128)(2,1)S(1)} %get-tuple-element.100), channel_id=1, source_target_pairs={{0,28},{2,30},{4,0},{6,2},{8,4},{10,6},{12,8},{14,10},{16,12},{18,... | collective-permute-start | bytes 786440 | tf_op jit(solution)/shard_map/ppermute | solution.py:23
  56.6 17.1 %collective-permute-start.17 = (bf16[384,768]{1,0:T(8,128)(2,1)S(1)}, bf16[384,768]{1,0:T(8,128)(2,1)S(1)}, u32[]{:S(2)}, u32[]{:S(2)}) collective-permute-start(bf16[384,768]{1,0:T(8,128)(2,1)S(1)} %get-tuple-element.106), channel_id=1, source_target_pairs={{0,1},{1,0},{2,3},{3,2},{4,5},{5,4},{6,7},{7,6},{8,9},{9,8},{10,11... | collective-permute-start | bytes 1769480 | tf_op jit(solution)/shard_map/ppermute | solution.py:23
  57.9 10.0 %collective-permute-start.16 = (bf16[144,512]{1,0:T(8,128)(2,1)S(1)}, bf16[144,512]{1,0:T(8,128)(2,1)S(1)}, u32[]{:S(2)}, u32[]{:S(2)}) collective-permute-start(bf16[144,512]{1,0:T(8,128)(2,1)S(1)} %get-tuple-element.115), channel_id=1, source_target_pairs={{0,4},{2,6},{4,8},{6,10},{8,12},{10,14},{12,16},{14,18},{16,20},{1... | collective-permute-start | bytes 442376 | tf_op jit(solution)/shard_map/ppermute | solution.py:23
  59.4 8.4 %collective-permute-start.15 = (bf16[144,512]{1,0:T(8,128)(2,1)S(1)}, bf16[144,512]{1,0:T(8,128)(2,1)S(1)}, u32[]{:S(2)}, u32[]{:S(2)}) collective-permute-start(bf16[144,512]{1,0:T(8,128)(2,1)S(1)} %get-tuple-element.114), channel_id=1, source_target_pairs={{0,2},{2,4},{4,6},{6,8},{8,10},{10,12},{12,14},{14,16},{16,18},{18... | collective-permute-start | bytes 442376 | tf_op jit(solution)/shard_map/ppermute | solution.py:23
  61.2 13.1 %collective-permute-start.13 = (bf16[128,1024]{1,0:T(8,128)(2,1)S(1)}, bf16[128,1024]{1,0:T(8,128)(2,1)S(1)}, u32[]{:S(2)}, u32[]{:S(2)}) collective-permute-start(bf16[128,1024]{1,0:T(8,128)(2,1)S(1)} %get-tuple-element.112), channel_id=1, source_target_pairs={{0,2},{2,4},{4,6},{6,8},{8,10},{10,12},{12,14},{14,16},{16,18},{18... | collective-permute-start | bytes 786440 | tf_op jit(solution)/shard_map/ppermute | solution.py:23
  61.3 13.0 %collective-permute-start.14 = (bf16[128,1024]{1,0:T(8,128)(2,1)S(1)}, bf16[128,1024]{1,0:T(8,128)(2,1)S(1)}, u32[]{:S(2)}, u32[]{:S(2)}) collective-permute-start(bf16[128,1024]{1,0:T(8,128)(2,1)S(1)} %get-tuple-element.113), channel_id=1, source_target_pairs={{0,4},{2,6},{4,8},{6,10},{8,12},{10,14},{12,16},{14,18},{16,20},{1... | collective-permute-start | bytes 786440 | tf_op jit(solution)/shard_map/ppermute | solution.py:23
  68.2 9.3 %collective-permute-start.20 = (bf16[208,512]{1,0:T(8,128)(2,1)S(1)}, bf16[208,512]{1,0:T(8,128)(2,1)S(1)}, u32[]{:S(2)}, u32[]{:S(2)}) collective-permute-start(bf16[208,512]{1,0:T(8,128)(2,1)S(1)} %grad_sent.2), channel_id=1, source_target_pairs={{0,1},{1,0},{2,3},{3,2},{4,5},{5,4},{6,7},{7,6},{8,9},{9,8},{10,11... | collective-permute-start | bytes 638984 | tf_op jit(solution)/shard_map/ppermute | solution.py:23
  73.8 10.2 %collective-permute-start.19 = (bf16[128,768]{1,0:T(8,128)(2,1)S(1)}, bf16[128,768]{1,0:T(8,128)(2,1)S(1)}, u32[]{:S(2)}, u32[]{:S(2)}) collective-permute-start(bf16[128,768]{1,0:T(8,128)(2,1)S(1)} %get-tuple-element.130), channel_id=1, source_target_pairs={{0,4},{2,6},{4,8},{6,10},{8,12},{10,14},{12,16},{14,18},{16,20},{1... | collective-permute-start | bytes 589832 | tf_op jit(solution)/shard_map/ppermute | solution.py:23
  73.9 10.2 %collective-permute-start.18 = (bf16[128,768]{1,0:T(8,128)(2,1)S(1)}, bf16[128,768]{1,0:T(8,128)(2,1)S(1)}, u32[]{:S(2)}, u32[]{:S(2)}) collective-permute-start(bf16[128,768]{1,0:T(8,128)(2,1)S(1)} %get-tuple-element.129), channel_id=1, source_target_pairs={{0,2},{2,4},{4,6},{6,8},{8,10},{10,12},{12,14},{14,16},{16,18},{18... | collective-permute-start | bytes 589832 | tf_op jit(solution)/shard_map/ppermute | solution.py:23
  74.9 11.5 %collective-permute-start.21 = (bf16[192,1024]{1,0:T(8,128)(2,1)S(1)}, bf16[192,1024]{1,0:T(8,128)(2,1)S(1)}, u32[]{:S(2)}, u32[]{:S(2)}) collective-permute-start(bf16[192,1024]{1,0:T(8,128)(2,1)S(1)} %mixed_sent.1), channel_id=1, source_target_pairs={{0,1},{1,0},{2,3},{3,2},{4,5},{5,4},{6,7},{7,6},{8,9},{9,8},{10,11... | collective-permute-start | bytes 1179656 | tf_op jit(solution)/shard_map/ppermute | solution.py:23
  84.5 8.8 %collective-permute-start.22 = (bf16[192,768]{1,0:T(8,128)(2,1)S(1)}, bf16[192,768]{1,0:T(8,128)(2,1)S(1)}, u32[]{:S(2)}, u32[]{:S(2)}) collective-permute-start(bf16[192,768]{1,0:T(8,128)(2,1)S(1)} %grad_sent.3), channel_id=1, source_target_pairs={{0,1},{1,0},{2,3},{3,2},{4,5},{5,4},{6,7},{7,6},{8,9},{9,8},{10,11... | collective-permute-start | bytes 884744 | tf_op jit(solution)/shard_map/ppermute | solution.py:23
where the time goes:
time: 94.3 us; the launch traced here: 94.1 us
  waiting for transfers between devices  37.5 us (40%)
  starting transfers between devices  33.5 us (36%)
  Pallas kernels  19.5 us (21%)
  local copies, waits for them, and re-layouts  2.72 us (3%)
  between operations  0.95 us (1%)
    ppermute x23, waiting for transfers between devices, shifted(): return lax.ppermute(value, axis, pairs)  37.5 us
    ppermute x23, starting transfers between devices, shifted(): return lax.ppermute(value, axis, pairs)  33.5 us
    pallas_call x24, Pallas kernels, run(): pl.pallas_call((lambda *refs: kernel(*refs[len(held):])) if held else ker...  19.5 us
    slice x5, local copies, waits for them, and re-layouts, on_device(): pieces.append((after(source, pieces[-1]) if pieces else source)[:, span(c)])  2.15 us
  transfers between devices with their start and end apart: 23, of which 10 were waited for; matrix products, arithmetic and copies ran while one was open for 1% of the time, Pallas kernels for 20%

commit v1 on v0

--- a/solution.py
+++ b/solution.py
@@ -28,36 +28,56 @@
 
 
 def whole(array):
-    return pl.BlockSpec(array.shape, lambda i: (0,) * len(array.shape))
+    return pl.BlockSpec(array.shape, lambda i, *_: (0,) * len(array.shape))
 
 
 def part(rows, columns, row, column):
-    return pl.BlockSpec((rows, columns), lambda i: (row, column))
+    return pl.BlockSpec((rows, columns), lambda i, *_: (row, column))
+
+
+def placed(rows, columns, row, column):
+    return pl.BlockSpec((pl.Element(rows), pl.Element(columns)), lambda i, *_: (row, column))
+
+
+def chosen(rows, columns):
+    return pl.BlockSpec((rows, columns), lambda i, scalar: (0, scalar[0]))
+
+
+def extent(spec):
+    rows, columns = (getattr(size, "block_size", size) for size in spec.block_shape)
+    return rows * columns
 
 
 class Steps:
     def __init__(self):
         self.last = None
 
-    def run(self, kernel, outs, operands, flops, name, held=(), tied=0, scale=SHARED):
+    def run(self, kernel, outs, operands, flops, name, held=(), tied=0, scale=SHARED, scalar=None):
         pair = lambda item: item if isinstance(item, tuple) else (item, whole(item))
         pairs = [pair(operand) for operand in operands]
         arrays, specs = [array for array, _ in pairs], [spec for _, spec in pairs]
         if self.last is not None:
             arrays[tied] = after(arrays[tied], self.last)
         out_shapes, out_specs = zip(*[pair(out) for out in outs])
-        moved = sum(2 * spec.block_shape[0] * spec.block_shape[1] for spec in specs + list(out_specs))
+        moved = sum(2 * extent(spec) for spec in specs + list(out_specs))
+        before = [] if scalar is None else [scalar]
+        skipped = len(before) + len(held)
         results = pl.pallas_call(
-            (lambda *refs: kernel(*refs[len(held) :])) if held else kernel,
-            grid=(1,),
+            (lambda *refs: kernel(*refs[skipped:])) if skipped else kernel,
+            grid_spec=pltpu.PrefetchScalarGridSpec(
+                num_scalar_prefetch=len(before),
+                grid=(1,),
+                in_specs=[pl.BlockSpec(memory_space=pl.ANY)] * len(held) + specs,
+                out_specs=out_specs,
+            ),
             out_shape=out_shapes,
-            in_specs=[pl.BlockSpec(memory_space=pl.ANY)] * len(held) + specs,
-            out_specs=out_specs,
-            input_output_aliases={i: i for i in range(len(held))},
+            input_output_aliases={len(before) + i: i for i in range(len(held))},
             compiler_params=pltpu.CompilerParams(vmem_limit_bytes=20 * 2**20),
-            cost_estimate=pl.CostEstimate(flops=int(flops * scale), bytes_accessed=int(moved * scale), transcendentals=0),
+            cost_estimate=pl.CostEstimate(
+                flops=int(flops * scale), bytes_accessed=int(moved * scale), transcendentals=0
+            ),
             name=name,
-        )(*held, *arrays)
+        )(*before, *held, *arrays)
         self.last = results[0]
         return results
 
@@ -218,11 +238,8 @@
     out[...] = total.astype(out.dtype)
 
 
-def join(me, own, arrived, out):
-    width = own.shape[1]
-    lower = me[0, 0] == 0
-    out[:, :width] = jnp.where(lower, own[...], arrived[...])
-    out[:, width:] = jnp.where(lower, arrived[...], own[...])
+def copy(source, out):
+    out[...] = source[...]
 
 
 def add_halves_and_gate(lists, kept, arrived, gate, out, gate_out):
@@ -256,6 +273,7 @@
     flops = 2 * total * width * hidden_units
 
     scalar = (me.reshape(1, 1), pl.BlockSpec((1, 1), lambda i: (0, 0), memory_space=pltpu.SMEM))
+    own_part, oth_part = me.reshape(1), (1 - me).reshape(1)
 
     def to_experts(rows):
         return [rows[0]] + [shifted(rows[s], "blk", -s) for s in range(1, lists)]
@@ -278,10 +296,11 @@
         operands = x[c] + out_grad[c] + [hidden, gate_grad, up_grad]
         return run(kernel(weight_grads), [rows_out, rows_out, columns_out], operands, 3 * flops, "w_grads", held=held)
 
-    def scatter(body, rows, values, gates, dtype, name, scale=BUSY):
-        extent = values[0].shape[1]
-        outs = [shape(count + values[0].shape[0] - cap, extent, dtype=dtype)]
-        return run(body, outs, [rows] + gates + values, 2 * total * count * extent, name, tied=-1, scale=scale)[0]
+    def scatter(body, rows, values, gates, dtype, name, scale=BUSY, out=None, **more):
+        columns = values[0].shape[1]
+        out = out or shape(count + values[0].shape[0] - cap, columns, dtype=dtype)
+        scatter_flops = 2 * total * count * columns
+        return run(body, [out], [rows] + gates + values, scatter_flops, name, tied=-1, scale=scale, **more)[0]
 
     pieces = []
     for source, c in [(tokens, 0), (tokens, 1), (cotangent, 0), (cotangent, 1)]:
@@ -318,10 +337,11 @@
         "hidden_grads",
         scale=BUSY,
     )
-    few, many = model // 4, model - model // 4
+    few = 3 * model // 8
+    many = model - few
     half = many // 2
     many_rows = lambda array: (array, part(many, hidden_units, 0, 0))
-    few_rows = lambda array: (array, part(few, hidden_units, many // few, 0))
+    few_rows = lambda array: (array, placed(few, hidden_units, many, 0))
     sent, second_kept = run(
         input_halves,
         [shape(total, half), shape(total, half, dtype=F32)],
@@ -342,7 +362,7 @@
     )
     first_rows = to_groups(rows)
     expert_out = to_groups(run(whole_rows, rows_shape, [kept, arrived], 0, "expert_out_rows"))
-    weight_outs = weights(1, weights(0, ()))
+    weight_outs = weights(0, ())
 
     half_shape = [shape(cap, half)] * lists
     sent = scatter(kernel(scatter_rows), oth_rows, first_rows, [], BF16, "grad_sent")
@@ -351,9 +371,11 @@
     first_kept = scatter(kernel(scatter_rows), own_rows, first_rows, [], F32, "grad_kept")
     sent = scatter(kernel(scatter_scaled), oth_column, expert_out, [oth_gate], BF16, "mixed_sent", SHARED)
     mixed_arrived = shifted(sent, "dp", 1)
-    mixed_own = scatter(kernel(scatter_scaled), own_column, expert_out, [own_gate], BF16, "mixed_own", SHARED)
-    few_columns = (shape(count, model), part(count, few, 0, many // few))
-    many_columns = (shape(count, model), part(count, many, 0, 0))
+    mixed_block = (shape(count, model), chosen(count, width))
+    mixed = scatter(
+        kernel(scatter_scaled), own_column, expert_out, [own_gate], BF16, "mixed_own", SHARED, mixed_block, scalar=own_part
+    )
+    few_columns = (shape(count, model), placed(count, few, 0, many))
     *grad, gate_out = run(
         kernel(add_halves_and_gate),
         [few_columns, shape(lists, count, dtype=F32)],
@@ -364,9 +386,13 @@
     )
     sent = scatter(kernel(scatter_rows), oth_rows, second_rows, [], BF16, "grad_sent")
     second_arrived = shifted(sent, "dp", 1)
-    second_own = scatter(kernel(scatter_rows), own_rows, second_rows, [], BF16, "grad_own")
-    mixed = run(join, [shape(count, model)], [scalar, mixed_own, mixed_arrived], 0, "mixed", tied=1, scale=BUSY)[0]
-    grad = run(join, [many_columns], [scalar, second_own, second_arrived], 0, "grad", held=grad, tied=1)[0]
+    many_block = (shape(count, model), chosen(count, half))
+    grad = scatter(
+        kernel(scatter_rows), own_rows, second_rows, [], BF16, "grad_own", out=many_block, held=grad, scalar=own_part
+    )
+    weight_outs = weights(1, weight_outs)
+    mixed = run(copy, [mixed_block], [mixed_arrived], 0, "mixed", held=[mixed], scale=BUSY, scalar=oth_part)[0]
+    grad = run(copy, [many_block], [second_arrived], 0, "grad", held=[grad], scalar=oth_part)[0]
     return (mixed, grad, gate_out.T) + tuple(out[None] for out in weight_outs)
 
 

time: 94.3 us -> 93.3 us (0.989); the launches traced: 94.1 us -> 92 us
  waiting for transfers between devices: 37.5 us -> 34.6 us
  Pallas kernels: 19.5 us -> 20.8 us
    ppermute x23, waiting for transfers between devices: 37.5 us -> 34.6 us  [shifted(): return lax.ppermute(value, axis, pairs)]
    pallas_call x24, Pallas kernels: 19.5 us -> 20.8 us  [run(): pl.pallas_call((lambda *refs: kernel(*refs[skipped:])) if skipped else ke...]
  transfers between devices with their start and end apart: 23 -> 23, of which waited for: 10 -> 13; matrix products, arithmetic and copies ran while one was open for 1% -> 1% of each run, Pallas kernels for 20% -> 22%
where the time goes in v1:
time: 93.3 us; the launch traced here: 92 us
  waiting for transfers between devices  34.6 us (37%)
  starting transfers between devices  32.9 us (35%)
  Pallas kernels  20.8 us (22%)
  local copies, waits for them, and re-layouts  2.72 us (3%)
    ppermute x23, waiting for transfers between devices, shifted(): return lax.ppermute(value, axis, pairs)  34.6 us
    ppermute x23, starting transfers between devices, shifted(): return lax.ppermute(value, axis, pairs)  32.9 us
    pallas_call x24, Pallas kernels, run(): pl.pallas_call((lambda *refs: kernel(*refs[skipped:])) if skipped else ke...  20.8 us
    slice x5, local copies, waits for them, and re-layouts, on_device(): pieces.append((after(source, pieces[-1]) if pieces else source)[:, span(c)])  2.15 us
  transfers between devices with their start and end apart: 23, of which 13 were waited for; matrix products, arithmetic and copies ran while one was open for 1% of the time, Pallas kernels for 22%

profile of v1, /device:TPU:0, one launch (start us, length us, event | category | flops | bytes accessed | tf_op | source)
XLA Modules:
  0.0 92.0 jit_solution(12782750997153440603)
XLA Ops:
  0.7 1.1 %slice.12 = bf16[192,1024]{1,0:T(8,128)(2,1)S(1)} slice(bf16[192,2048]{1,0:T(8,128)(2,1)} %own.5), slice={[0:192], [0:1024]} | slice | bytes 786432 | tf_op jit(solution)/shard_map/slice | solution.py:307
  1.8 3.0 %collective-permute-start.1 = (bf16[192,1024]{1,0:T(8,128)(2,1)S(1)}, bf16[192,1024]{1,0:T(8,128)(2,1)S(1)}, u32[]{:S(2)}, u32[]{:S(2)}) collective-permute-start(bf16[192,1024]{1,0:T(8,128)(2,1)S(1)} %slice.12), channel_id=1, source_target_pairs={{0,1},{1,0},{2,3},{3,2},{4,5},{5,4},{6,7},{7,6},{8,9},{9,8},{10,11... | collective-permute-start | bytes 1179656 | tf_op jit(solution)/shard_map/ppermute | solution.py:23
  4.8 1.0 %slice.13 = bf16[192,1024]{1,0:T(8,128)(2,1)S(1)} slice(bf16[192,2048]{1,0:T(8,128)(2,1)} %own.5), slice={[0:192], [1024:2048]} | slice | bytes 786432 | tf_op jit(solution)/shard_map/slice | solution.py:307
  6.3 8.5 %collective-permute-done.1.oth = bf16[192,1024]{1,0:T(8,128)(2,1)S(1)} collective-permute-done((bf16[192,1024]{1,0:T(8,128)(2,1)S(1)}, bf16[192,1024]{1,0:T(8,128)(2,1)S(1)}, u32[]{:S(2)}, u32[]{:S(2)}) %collective-permute-start.1) | collective-permute-done | bytes 393248 | tf_op jit(solution)/shard_map/ppermute | solution.py:23
  15.4 2.5 %collective-permute-start.3 = (bf16[128,1024]{1,0:T(8,128)(2,1)S(1)}, bf16[128,1024]{1,0:T(8,128)(2,1)S(1)}, u32[]{:S(2)}, u32[]{:S(2)}) collective-permute-start(bf16[128,1024]{1,0:T(8,128)(2,1)S(1)} %get-tuple-element.79), channel_id=1, source_target_pairs={{0,30},{2,0},{4,2},{6,4},{8,6},{10,8},{12,10},{14,12},{16,14},{18,... | collective-permute-start | bytes 786440 | tf_op jit(solution)/shard_map/ppermute | solution.py:23
  17.9 1.6 %collective-permute-start.2 = (bf16[208,1024]{1,0:T(8,128)(2,1)S(1)}, bf16[208,1024]{1,0:T(8,128)(2,1)S(1)}, u32[]{:S(2)}, u32[]{:S(2)}) collective-permute-start(bf16[208,1024]{1,0:T(8,128)(2,1)S(1)} %fusion.1), channel_id=1, source_target_pairs={{0,1},{1,0},{2,3},{3,2},{4,5},{5,4},{6,7},{7,6},{8,9},{9,8},{10,11... | collective-permute-start | bytes 1277960 | tf_op jit(solution)/shard_map/ppermute | solution.py:23
  19.5 2.6 %collective-permute-start.4 = (bf16[128,1024]{1,0:T(8,128)(2,1)S(1)}, bf16[128,1024]{1,0:T(8,128)(2,1)S(1)}, u32[]{:S(2)}, u32[]{:S(2)}) collective-permute-start(bf16[128,1024]{1,0:T(8,128)(2,1)S(1)} %get-tuple-element.80), channel_id=1, source_target_pairs={{0,28},{2,30},{4,0},{6,2},{8,4},{10,6},{12,8},{14,10},{16,12},{18,... | collective-permute-start | bytes 786440 | tf_op jit(solution)/shard_map/ppermute | solution.py:23
  23.8 2.5 %collective-permute-start.5 = (bf16[128,1024]{1,0:T(8,128)(2,1)S(1)}, bf16[128,1024]{1,0:T(8,128)(2,1)S(1)}, u32[]{:S(2)}, u32[]{:S(2)}) collective-permute-start(bf16[128,1024]{1,0:T(8,128)(2,1)S(1)} %get-tuple-element.85), channel_id=1, source_target_pairs={{0,30},{2,0},{4,2},{6,4},{8,6},{10,8},{12,10},{14,12},{16,14},{18,... | collective-permute-start | bytes 786440 | tf_op jit(solution)/shard_map/ppermute | solution.py:23
  26.3 2.7 %collective-permute-start.6 = (bf16[128,1024]{1,0:T(8,128)(2,1)S(1)}, bf16[128,1024]{1,0:T(8,128)(2,1)S(1)}, u32[]{:S(2)}, u32[]{:S(2)}) collective-permute-start(bf16[128,1024]{1,0:T(8,128)(2,1)S(1)} %get-tuple-element.86), channel_id=1, source_target_pairs={{0,28},{2,30},{4,0},{6,2},{8,4},{10,6},{12,8},{14,10},{16,12},{18,... | collective-permute-start | bytes 786440 | tf_op jit(solution)/shard_map/ppermute | solution.py:23
  30.0 2.3 %collective-permute-done.2.oth.oth_gate.gate = bf16[208,1024]{1,0:T(8,128)(2,1)S(1)} collective-permute-done((bf16[208,1024]{1,0:T(8,128)(2,1)S(1)}, bf16[208,1024]{1,0:T(8,128)(2,1)S(1)}, u32[]{:S(2)}, u32[]{:S(2)}) %collective-permute-start.2) | collective-permute-done | bytes 426016 | tf_op jit(solution)/shard_map/ppermute | solution.py:23
  33.0 2.5 %collective-permute-start.8 = (bf16[128,1024]{1,0:T(8,128)(2,1)S(1)}, bf16[128,1024]{1,0:T(8,128)(2,1)S(1)}, u32[]{:S(2)}, u32[]{:S(2)}) collective-permute-start(bf16[128,1024]{1,0:T(8,128)(2,1)S(1)} %get-tuple-element.96), channel_id=1, source_target_pairs={{0,30},{2,0},{4,2},{6,4},{8,6},{10,8},{12,10},{14,12},{16,14},{18,... | collective-permute-start | bytes 786440 | tf_op jit(solution)/shard_map/ppermute | solution.py:23
  35.6 2.7 %collective-permute-start.9 = (bf16[128,1024]{1,0:T(8,128)(2,1)S(1)}, bf16[128,1024]{1,0:T(8,128)(2,1)S(1)}, u32[]{:S(2)}, u32[]{:S(2)}) collective-permute-start(bf16[128,1024]{1,0:T(8,128)(2,1)S(1)} %get-tuple-element.97), channel_id=1, source_target_pairs={{0,28},{2,30},{4,0},{6,2},{8,4},{10,6},{12,8},{14,10},{16,12},{18,... | collective-permute-start | bytes 786440 | tf_op jit(solution)/shard_map/ppermute | solution.py:23
  38.2 1.2 %hidden.1 = (bf16[384,384]{1,0:T(8,128)(2,1)S(1)}, f32[384,384]{1,0:T(8,128)S(1)}, f32[384,384]{1,0:T(8,128)S(1)}) custom-call(bf16[128,1024]{1,0:T(8,128)(2,1)S(1)} %get-tuple-element.133.refs_0_.refs_3_, bf16[128,1024]{1,0:T(8,128)(2,1)S(1)} %collective-permute-done.5.refs_1_.refs_4_, bf16[128,1024]{1,0:T(8,128)(2,1)S(1)} %collective-permute-done.6.refs_2_.refs_5_, ...), custom_call_target="tpu_custom_call" | custom-call | flops 6039797 | bytes 38338 | tf_op jit(solution)/shard_map/hidden/pallas_call | solution.py:65
  40.6 1.6 %collective-permute-start.12 = (bf16[384,1024]{1,0:T(8,128)(2,1)S(1)}, bf16[384,1024]{1,0:T(8,128)(2,1)S(1)}, u32[]{:S(2)}, u32[]{:S(2)}) collective-permute-start(bf16[384,1024]{1,0:T(8,128)(2,1)S(1)} %get-tuple-element.92), channel_id=1, source_target_pairs={{0,1},{1,0},{2,3},{3,2},{4,5},{5,4},{6,7},{7,6},{8,9},{9,8},{10,11... | collective-permute-start | bytes 2359304 | tf_op jit(solution)/shard_map/ppermute | solution.py:23
  42.9 1.7 %collective-permute-start.10 = (bf16[128,1024]{1,0:T(8,128)(2,1)S(1)}, bf16[128,1024]{1,0:T(8,128)(2,1)S(1)}, u32[]{:S(2)}, u32[]{:S(2)}) collective-permute-start(bf16[128,1024]{1,0:T(8,128)(2,1)S(1)} %get-tuple-element.99), channel_id=1, source_target_pairs={{0,30},{2,0},{4,2},{6,4},{8,6},{10,8},{12,10},{14,12},{16,14},{18,... | collective-permute-start | bytes 786440 | tf_op jit(solution)/shard_map/ppermute | solution.py:23
  44.6 1.3 %collective-permute-start.11 = (bf16[128,1024]{1,0:T(8,128)(2,1)S(1)}, bf16[128,1024]{1,0:T(8,128)(2,1)S(1)}, u32[]{:S(2)}, u32[]{:S(2)}) collective-permute-start(bf16[128,1024]{1,0:T(8,128)(2,1)S(1)} %get-tuple-element.100), channel_id=1, source_target_pairs={{0,28},{2,30},{4,0},{6,2},{8,4},{10,6},{12,8},{14,10},{16,12},{18,... | collective-permute-start | bytes 786440 | tf_op jit(solution)/shard_map/ppermute | solution.py:23
  46.4 4.2 %collective-permute-done.10.refs_1_.refs_7_ = bf16[128,1024]{1,0:T(8,128)(2,1)S(1)} collective-permute-done((bf16[128,1024]{1,0:T(8,128)(2,1)S(1)}, bf16[128,1024]{1,0:T(8,128)(2,1)S(1)}, u32[]{:S(2)}, u32[]{:S(2)}) %collective-permute-start.10) | collective-permute-done | bytes 262176 | tf_op jit(solution)/shard_map/ppermute | solution.py:23
  50.6 3.9 %collective-permute-done.11.refs_2_.refs_8_ = bf16[128,1024]{1,0:T(8,128)(2,1)S(1)} collective-permute-done((bf16[128,1024]{1,0:T(8,128)(2,1)S(1)}, bf16[128,1024]{1,0:T(8,128)(2,1)S(1)}, u32[]{:S(2)}, u32[]{:S(2)}) %collective-permute-start.11) | collective-permute-done | bytes 262176 | tf_op jit(solution)/shard_map/ppermute | solution.py:23
  55.2 1.4 %input_grad.2 = (bf16[384,640]{1,0:T(8,128)(2,1)S(1)}, f32[384,640]{1,0:T(8,128)S(1)}) custom-call(s32[1,1]{1,0:T(1,128)} %bitcast.3.me, bf16[384,384]{1,0:T(8,128)(2,1)S(1)} %get-tuple-element.107.gate_grad.refs_7_.refs_10_, bf16[384,384]{1,0:T(8,128)(2,1)S(1)} %get-tuple-element.105.up_grad.refs_8_.refs_11_, bf16[2048,384]{1,0:T(8,128)(2,1)S(1)} %bitcast.36, ...), custom_call_target="tpu_custom_call" | custom-call | flops 9059696640 | bytes 35389460 | tf_op jit(solution)/shard_map/input_grad/pallas_call | solution.py:65
  58.0 1.6 %collective-permute-start.16 = (bf16[144,768]{1,0:T(8,128)(2,1)S(1)}, bf16[144,768]{1,0:T(8,128)(2,1)S(1)}, u32[]{:S(2)}, u32[]{:S(2)}) collective-permute-start(bf16[144,768]{1,0:T(8,128)(2,1)S(1)} %get-tuple-element.115), channel_id=1, source_target_pairs={{0,4},{2,6},{4,8},{6,10},{8,12},{10,14},{12,16},{14,18},{16,20},{1... | collective-permute-start | bytes 663560 | tf_op jit(solution)/shard_map/ppermute | solution.py:23
  59.6 1.5 %collective-permute-done.12.arrived = bf16[384,1024]{1,0:T(8,128)(2,1)S(1)} collective-permute-done((bf16[384,1024]{1,0:T(8,128)(2,1)S(1)}, bf16[384,1024]{1,0:T(8,128)(2,1)S(1)}, u32[]{:S(2)}, u32[]{:S(2)}) %collective-permute-start.12) | collective-permute-done | bytes 786464 | tf_op jit(solution)/shard_map/ppermute | solution.py:23
  61.4 1.6 %collective-permute-start.14 = (bf16[128,1024]{1,0:T(8,128)(2,1)S(1)}, bf16[128,1024]{1,0:T(8,128)(2,1)S(1)}, u32[]{:S(2)}, u32[]{:S(2)}) collective-permute-start(bf16[128,1024]{1,0:T(8,128)(2,1)S(1)} %get-tuple-element.113), channel_id=1, source_target_pairs={{0,4},{2,6},{4,8},{6,10},{8,12},{10,14},{12,16},{14,18},{16,20},{1... | collective-permute-start | bytes 786440 | tf_op jit(solution)/shard_map/ppermute | solution.py:23
  62.9 2.4 %w_grads.2 = (bf16[2048,384]{1,0:T(8,128)(2,1)}, bf16[2048,384]{1,0:T(8,128)(2,1)}, bf16[384,2048]{1,0:T(8,128)(2,1)}) custom-call(bf16[128,1024]{1,0:T(8,128)(2,1)S(1)} %get-tuple-element.117.refs_0_, bf16[128,1024]{1,0:T(8,128)(2,1)S(1)} %collective-permute-done.3.refs_1_, bf16[128,1024]{1,0:T(8,128)(2,1)S(1)} %collective-permute-done.4.refs_2_, ...), custom_call_target="tpu_custom_call" | custom-call | flops 9059696 | bytes 48168 | tf_op jit(solution)/shard_map/w_grads/pallas_call | solution.py:65
  65.4 3.7 %collective-permute-done.16.refs_2_ = bf16[144,768]{1,0:T(8,128)(2,1)S(1)} collective-permute-done((bf16[144,768]{1,0:T(8,128)(2,1)S(1)}, bf16[144,768]{1,0:T(8,128)(2,1)S(1)}, u32[]{:S(2)}, u32[]{:S(2)}) %collective-permute-start.16) | collective-permute-done | bytes 221216 | tf_op jit(solution)/shard_map/ppermute | solution.py:23
  72.4 2.3 %collective-permute-done.14.refs_2_.refs_5_ = bf16[128,1024]{1,0:T(8,128)(2,1)S(1)} collective-permute-done((bf16[128,1024]{1,0:T(8,128)(2,1)S(1)}, bf16[128,1024]{1,0:T(8,128)(2,1)S(1)}, u32[]{:S(2)}, u32[]{:S(2)}) %collective-permute-start.14) | collective-permute-done | bytes 262176 | tf_op jit(solution)/shard_map/ppermute | solution.py:23
  75.7 1.2 %collective-permute-start.18 = (bf16[192,1024]{1,0:T(8,128)(2,1)S(1)}, bf16[192,1024]{1,0:T(8,128)(2,1)S(1)}, u32[]{:S(2)}, u32[]{:S(2)}) collective-permute-start(bf16[192,1024]{1,0:T(8,128)(2,1)S(1)} %mixed_sent.1), channel_id=1, source_target_pairs={{0,1},{1,0},{2,3},{3,2},{4,5},{5,4},{6,7},{7,6},{8,9},{9,8},{10,11... | collective-permute-start | bytes 1179656 | tf_op jit(solution)/shard_map/ppermute | solution.py:23
  76.9 1.3 %mixed_own.1.refs_1_ = bf16[192,2048]{1,0:T(8,128)(2,1)} custom-call(s32[1]{0:T(128)} %bitcast.1.refs_0_, s32[384,1]{1,0:T(8,128)S(1)} %bitcast.33, f32[3,192]{1,0:T(4,128)S(1)} %bitcast_convert_fusion.own_gate.refs_2_.gate, bf16[128,1024]{1,0:T(8,128)(2,1)S(1)} %get-tuple-element.111.refs_0_.refs_3_, ...), custom_call_target="tpu_custom_call" | custom-call | flops 1509949 | bytes 11815 | tf_op jit(solution)/shard_map/mixed_own/pallas_call | solution.py:65
  79.0 2.9 %collective-permute-done.21.refs_2_.refs_5_ = bf16[128,640]{1,0:T(8,128)(2,1)S(1)} collective-permute-done((bf16[128,640]{1,0:T(8,128)(2,1)S(1)}, bf16[128,640]{1,0:T(8,128)(2,1)S(1)}, u32[]{:S(2)}, u32[]{:S(2)}) %collective-permute-start.21) | collective-permute-done | bytes 163872 | tf_op jit(solution)/shard_map/ppermute | solution.py:23
  82.2 1.5 %collective-permute-start.22 = (bf16[192,640]{1,0:T(8,128)(2,1)S(1)}, bf16[192,640]{1,0:T(8,128)(2,1)S(1)}, u32[]{:S(2)}, u32[]{:S(2)}) collective-permute-start(bf16[192,640]{1,0:T(8,128)(2,1)S(1)} %grad_sent.3), channel_id=1, source_target_pairs={{0,1},{1,0},{2,3},{3,2},{4,5},{5,4},{6,7},{7,6},{8,9},{9,8},{10,11... | collective-permute-start | bytes 737288 | tf_op jit(solution)/shard_map/ppermute | solution.py:23
  83.7 1.0 %grad_own.1.refs_1_ = bf16[192,2048]{1,0:T(8,128)(2,1)} custom-call(s32[1]{0:T(128)} %bitcast.1.refs_0_, bf16[192,2048]{1,0:T(8,128)(2,1)} %get-tuple-element.128.refs_1_, s32[3,128]{1,0:T(4,128)S(1)} %get-tuple-element.141.rows.refs_2_, bf16[128,640]{1,0:T(8,128)(2,1)S(1)} %get-tuple-element.121.refs_0_.refs_3_, ...), custom_call_target="tpu_custom_call", output_to_operand_aliasing={{}: (1, {})} | custom-call | flops 943718400 | bytes 7380480 | tf_op jit(solution)/shard_map/grad_own/pallas_call | solution.py:65
  84.7 2.6 %w_grads.3 = (bf16[2048,384]{1,0:T(8,128)(2,1)}, bf16[2048,384]{1,0:T(8,128)(2,1)}, bf16[384,2048]{1,0:T(8,128)(2,1)}) custom-call(bf16[2048,384]{1,0:T(8,128)(2,1)} %get-tuple-element.118.refs_0_, bf16[2048,384]{1,0:T(8,128)(2,1)} %get-tuple-element.125.refs_1_, ...), custom_call_target="tpu_custom_call", output_to_operand_aliasing={{0}: (0, {}), {1}: (1, {}), {2}: (2, {})} | custom-call | flops 9059696 | bytes 48168 | tf_op jit(solution)/shard_map/w_grads/pallas_call | solution.py:65
  88.1 3.2 %collective-permute-done.22.refs_2_ = bf16[192,640]{1,0:T(8,128)(2,1)S(1)} collective-permute-done((bf16[192,640]{1,0:T(8,128)(2,1)S(1)}, bf16[192,640]{1,0:T(8,128)(2,1)S(1)}, u32[]{:S(2)}, u32[]{:S(2)}) %collective-permute-start.22) | collective-permute-done | bytes 245792 | tf_op jit(solution)/shard_map/ppermute | solution.py:23
  (64 shorter events, 16.3 us)
Async XLA Ops:
  0.6 14.1 %copy-start = (bf16[192,2048]{1,0:T(8,128)(2,1)S(1)}, bf16[192,2048]{1,0:T(8,128)(2,1)}, u32[]{:S(2)}) copy-start(bf16[192,2048]{1,0:T(8,128)(2,1)} %own.5) | copy-start | bytes 2359300
  0.6 5.3 %copy-start.6 = (s32[3,128]{1,0:T(4,128)S(1)}, s32[3,128]{1,0:T(4,128)}, u32[]{:S(2)}) copy-start(s32[3,128]{1,0:T(4,128)} %param.10) | copy-start | bytes 4612
  1.8 13.0 %collective-permute-start.1 = (bf16[192,1024]{1,0:T(8,128)(2,1)S(1)}, bf16[192,1024]{1,0:T(8,128)(2,1)S(1)}, u32[]{:S(2)}, u32[]{:S(2)}) collective-permute-start(bf16[192,1024]{1,0:T(8,128)(2,1)S(1)} %slice.12), channel_id=1, source_target_pairs={{0,1},{1,0},{2,3},{3,2},{4,5},{5,4},{6,7},{7,6},{8,9},{9,8},{10,11... | collective-permute-start | bytes 1179656 | tf_op jit(solution)/shard_map/ppermute | solution.py:23
  5.8 12.1 %slice-start = ((bf16[192,2048]{1,0:T(8,128)(2,1)}), bf16[192,1024]{1,0:T(8,128)(2,1)S(1)}, s32[]{:S(2)}) async-start(bf16[192,2048]{1,0:T(8,128)(2,1)} %own.7), calls=%async_computation | async-start | bytes 786432 | tf_op jit(solution)/shard_map/slice | solution.py:307
  5.8 12.1 %copy-start.5 = (bf16[192,3]{0,1:T(4,128)(2,1)S(1)}, bf16[192,3]{0,1:T(4,128)(2,1)}, u32[]{:S(2)}) copy-start(bf16[192,3]{0,1:T(4,128)(2,1)} %param.9) | copy-start | bytes 3460
  5.8 17.3 %collective-permute-start = (bf16[192,1024]{1,0:T(8,128)(2,1)S(1)}, bf16[192,1024]{1,0:T(8,128)(2,1)S(1)}, u32[]{:S(2)}, u32[]{:S(2)}) collective-permute-start(bf16[192,1024]{1,0:T(8,128)(2,1)S(1)} %slice.13), channel_id=1, source_target_pairs={{0,1},{1,0},{2,3},{3,2},{4,5},{5,4},{6,7},{7,6},{8,9},{9,8},{10,11... | collective-permute-start | bytes 1179656 | tf_op jit(solution)/shard_map/ppermute | solution.py:23
  6.3 15.9 %copy-start.1 = (bf16[192,2048]{1,0:T(8,128)(2,1)S(1)}, bf16[192,2048]{1,0:T(8,128)(2,1)}, u32[]{:S(2)}) copy-start(bf16[192,2048]{1,0:T(8,128)(2,1)} %own.7) | copy-start | bytes 2359300
  15.4 11.0 %collective-permute-start.3 = (bf16[128,1024]{1,0:T(8,128)(2,1)S(1)}, bf16[128,1024]{1,0:T(8,128)(2,1)S(1)}, u32[]{:S(2)}, u32[]{:S(2)}) collective-permute-start(bf16[128,1024]{1,0:T(8,128)(2,1)S(1)} %get-tuple-element.79), channel_id=1, source_target_pairs={{0,30},{2,0},{4,2},{6,4},{8,6},{10,8},{12,10},{14,12},{16,14},{18,... | collective-permute-start | bytes 786440 | tf_op jit(solution)/shard_map/ppermute | solution.py:23
  17.9 11.1 %copy-start.2 = (bf16[1,2048,384]{2,1,0:T(8,128)(2,1)S(1)}, bf16[1,2048,384]{2,1,0:T(8,128)(2,1)}, u32[]{:S(2)}) copy-start(bf16[1,2048,384]{2,1,0:T(8,128)(2,1)} %param.11) | copy-start | bytes 4718596
  17.9 11.1 %copy-start.3 = (bf16[1,2048,384]{2,1,0:T(8,128)(2,1)S(1)}, bf16[1,2048,384]{2,1,0:T(8,128)(2,1)}, u32[]{:S(2)}) copy-start(bf16[1,2048,384]{2,1,0:T(8,128)(2,1)} %param.12) | copy-start | bytes 4718596
  17.9 14.3 %collective-permute-start.2 = (bf16[208,1024]{1,0:T(8,128)(2,1)S(1)}, bf16[208,1024]{1,0:T(8,128)(2,1)S(1)}, u32[]{:S(2)}, u32[]{:S(2)}) collective-permute-start(bf16[208,1024]{1,0:T(8,128)(2,1)S(1)} %fusion.1), channel_id=1, source_target_pairs={{0,1},{1,0},{2,3},{3,2},{4,5},{5,4},{6,7},{7,6},{8,9},{9,8},{10,11... | collective-permute-start | bytes 1277960 | tf_op jit(solution)/shard_map/ppermute | solution.py:23
  19.5 9.4 %collective-permute-start.4 = (bf16[128,1024]{1,0:T(8,128)(2,1)S(1)}, bf16[128,1024]{1,0:T(8,128)(2,1)S(1)}, u32[]{:S(2)}, u32[]{:S(2)}) collective-permute-start(bf16[128,1024]{1,0:T(8,128)(2,1)S(1)} %get-tuple-element.80), channel_id=1, source_target_pairs={{0,28},{2,30},{4,0},{6,2},{8,4},{10,6},{12,8},{14,10},{16,12},{18,... | collective-permute-start | bytes 786440 | tf_op jit(solution)/shard_map/ppermute | solution.py:23
  22.2 20.0 %collective-permute-start.7 = (bf16[192,1024]{1,0:T(8,128)(2,1)S(1)}, bf16[192,1024]{1,0:T(8,128)(2,1)S(1)}, u32[]{:S(2)}, u32[]{:S(2)}) collective-permute-start(bf16[192,1024]{1,0:T(8,128)(2,1)S(1)} %slice.15), channel_id=1, source_target_pairs={{0,1},{1,0},{2,3},{3,2},{4,5},{5,4},{6,7},{7,6},{8,9},{9,8},{10,11... | collective-permute-start | bytes 1179656 | tf_op jit(solution)/shard_map/ppermute | solution.py:23
  23.8 14.4 %collective-permute-start.5 = (bf16[128,1024]{1,0:T(8,128)(2,1)S(1)}, bf16[128,1024]{1,0:T(8,128)(2,1)S(1)}, u32[]{:S(2)}, u32[]{:S(2)}) collective-permute-start(bf16[128,1024]{1,0:T(8,128)(2,1)S(1)} %get-tuple-element.85), channel_id=1, source_target_pairs={{0,30},{2,0},{4,2},{6,4},{8,6},{10,8},{12,10},{14,12},{16,14},{18,... | collective-permute-start | bytes 786440 | tf_op jit(solution)/shard_map/ppermute | solution.py:23
  26.3 11.9 %collective-permute-start.6 = (bf16[128,1024]{1,0:T(8,128)(2,1)S(1)}, bf16[128,1024]{1,0:T(8,128)(2,1)S(1)}, u32[]{:S(2)}, u32[]{:S(2)}) collective-permute-start(bf16[128,1024]{1,0:T(8,128)(2,1)S(1)} %get-tuple-element.86), channel_id=1, source_target_pairs={{0,28},{2,30},{4,0},{6,2},{8,4},{10,6},{12,8},{14,10},{16,12},{18,... | collective-permute-start | bytes 786440 | tf_op jit(solution)/shard_map/ppermute | solution.py:23
  33.0 12.8 %collective-permute-start.8 = (bf16[128,1024]{1,0:T(8,128)(2,1)S(1)}, bf16[128,1024]{1,0:T(8,128)(2,1)S(1)}, u32[]{:S(2)}, u32[]{:S(2)}) collective-permute-start(bf16[128,1024]{1,0:T(8,128)(2,1)S(1)} %get-tuple-element.96), channel_id=1, source_target_pairs={{0,30},{2,0},{4,2},{6,4},{8,6},{10,8},{12,10},{14,12},{16,14},{18,... | collective-permute-start | bytes 786440 | tf_op jit(solution)/shard_map/ppermute | solution.py:23
  35.6 10.3 %collective-permute-start.9 = (bf16[128,1024]{1,0:T(8,128)(2,1)S(1)}, bf16[128,1024]{1,0:T(8,128)(2,1)S(1)}, u32[]{:S(2)}, u32[]{:S(2)}) collective-permute-start(bf16[128,1024]{1,0:T(8,128)(2,1)S(1)} %get-tuple-element.97), channel_id=1, source_target_pairs={{0,28},{2,30},{4,0},{6,2},{8,4},{10,6},{12,8},{14,10},{16,12},{18,... | collective-permute-start | bytes 786440 | tf_op jit(solution)/shard_map/ppermute | solution.py:23
  38.2 1.4 %copy-start.4 = (bf16[1,384,2048]{2,1,0:T(8,128)(2,1)S(1)}, bf16[1,384,2048]{2,1,0:T(8,128)(2,1)}, u32[]{:S(2)}) copy-start(bf16[1,384,2048]{2,1,0:T(8,128)(2,1)} %param.13) | copy-start | bytes 4718596
  40.6 20.4 %collective-permute-start.12 = (bf16[384,1024]{1,0:T(8,128)(2,1)S(1)}, bf16[384,1024]{1,0:T(8,128)(2,1)S(1)}, u32[]{:S(2)}, u32[]{:S(2)}) collective-permute-start(bf16[384,1024]{1,0:T(8,128)(2,1)S(1)} %get-tuple-element.92), channel_id=1, source_target_pairs={{0,1},{1,0},{2,3},{3,2},{4,5},{5,4},{6,7},{7,6},{8,9},{9,8},{10,11... | collective-permute-start | bytes 2359304 | tf_op jit(solution)/shard_map/ppermute | solution.py:23
  42.9 7.7 %collective-permute-start.10 = (bf16[128,1024]{1,0:T(8,128)(2,1)S(1)}, bf16[128,1024]{1,0:T(8,128)(2,1)S(1)}, u32[]{:S(2)}, u32[]{:S(2)}) collective-permute-start(bf16[128,1024]{1,0:T(8,128)(2,1)S(1)} %get-tuple-element.99), channel_id=1, source_target_pairs={{0,30},{2,0},{4,2},{6,4},{8,6},{10,8},{12,10},{14,12},{16,14},{18,... | collective-permute-start | bytes 786440 | tf_op jit(solution)/shard_map/ppermute | solution.py:23
  44.6 9.9 %collective-permute-start.11 = (bf16[128,1024]{1,0:T(8,128)(2,1)S(1)}, bf16[128,1024]{1,0:T(8,128)(2,1)S(1)}, u32[]{:S(2)}, u32[]{:S(2)}) collective-permute-start(bf16[128,1024]{1,0:T(8,128)(2,1)S(1)} %get-tuple-element.100), channel_id=1, source_target_pairs={{0,28},{2,30},{4,0},{6,2},{8,4},{10,6},{12,8},{14,10},{16,12},{18,... | collective-permute-start | bytes 786440 | tf_op jit(solution)/shard_map/ppermute | solution.py:23
  56.6 15.0 %collective-permute-start.17 = (bf16[384,640]{1,0:T(8,128)(2,1)S(1)}, bf16[384,640]{1,0:T(8,128)(2,1)S(1)}, u32[]{:S(2)}, u32[]{:S(2)}) collective-permute-start(bf16[384,640]{1,0:T(8,128)(2,1)S(1)} %get-tuple-element.106), channel_id=1, source_target_pairs={{0,1},{1,0},{2,3},{3,2},{4,5},{5,4},{6,7},{7,6},{8,9},{9,8},{10,11... | collective-permute-start | bytes 1474568 | tf_op jit(solution)/shard_map/ppermute | solution.py:23
  58.0 11.1 %collective-permute-start.16 = (bf16[144,768]{1,0:T(8,128)(2,1)S(1)}, bf16[144,768]{1,0:T(8,128)(2,1)S(1)}, u32[]{:S(2)}, u32[]{:S(2)}) collective-permute-start(bf16[144,768]{1,0:T(8,128)(2,1)S(1)} %get-tuple-element.115), channel_id=1, source_target_pairs={{0,4},{2,6},{4,8},{6,10},{8,12},{10,14},{12,16},{14,18},{16,20},{1... | collective-permute-start | bytes 663560 | tf_op jit(solution)/shard_map/ppermute | solution.py:23
  59.6 10.3 %collective-permute-start.15 = (bf16[144,768]{1,0:T(8,128)(2,1)S(1)}, bf16[144,768]{1,0:T(8,128)(2,1)S(1)}, u32[]{:S(2)}, u32[]{:S(2)}) collective-permute-start(bf16[144,768]{1,0:T(8,128)(2,1)S(1)} %get-tuple-element.114), channel_id=1, source_target_pairs={{0,2},{2,4},{4,6},{6,8},{8,10},{10,12},{12,14},{14,16},{16,18},{18... | collective-permute-start | bytes 663560 | tf_op jit(solution)/shard_map/ppermute | solution.py:23
  61.2 13.9 %collective-permute-start.13 = (bf16[128,1024]{1,0:T(8,128)(2,1)S(1)}, bf16[128,1024]{1,0:T(8,128)(2,1)S(1)}, u32[]{:S(2)}, u32[]{:S(2)}) collective-permute-start(bf16[128,1024]{1,0:T(8,128)(2,1)S(1)} %get-tuple-element.112), channel_id=1, source_target_pairs={{0,2},{2,4},{4,6},{6,8},{8,10},{10,12},{12,14},{14,16},{16,18},{18... | collective-permute-start | bytes 786440 | tf_op jit(solution)/shard_map/ppermute | solution.py:23
  61.4 13.3 %collective-permute-start.14 = (bf16[128,1024]{1,0:T(8,128)(2,1)S(1)}, bf16[128,1024]{1,0:T(8,128)(2,1)S(1)}, u32[]{:S(2)}, u32[]{:S(2)}) collective-permute-start(bf16[128,1024]{1,0:T(8,128)(2,1)S(1)} %get-tuple-element.113), channel_id=1, source_target_pairs={{0,4},{2,6},{4,8},{6,10},{8,12},{10,14},{12,16},{14,18},{16,20},{1... | collective-permute-start | bytes 786440 | tf_op jit(solution)/shard_map/ppermute | solution.py:23
  70.3 7.8 %collective-permute-start.19 = (bf16[208,768]{1,0:T(8,128)(2,1)S(1)}, bf16[208,768]{1,0:T(8,128)(2,1)S(1)}, u32[]{:S(2)}, u32[]{:S(2)}) collective-permute-start(bf16[208,768]{1,0:T(8,128)(2,1)S(1)} %grad_sent.2), channel_id=1, source_target_pairs={{0,1},{1,0},{2,3},{3,2},{4,5},{5,4},{6,7},{7,6},{8,9},{9,8},{10,11... | collective-permute-start | bytes 958472 | tf_op jit(solution)/shard_map/ppermute | solution.py:23
  71.7 10.1 %collective-permute-start.20 = (bf16[128,640]{1,0:T(8,128)(2,1)S(1)}, bf16[128,640]{1,0:T(8,128)(2,1)S(1)}, u32[]{:S(2)}, u32[]{:S(2)}) collective-permute-start(bf16[128,640]{1,0:T(8,128)(2,1)S(1)} %get-tuple-element.129), channel_id=1, source_target_pairs={{0,2},{2,4},{4,6},{6,8},{8,10},{10,12},{12,14},{14,16},{16,18},{18... | collective-permute-start | bytes 491528 | tf_op jit(solution)/shard_map/ppermute | solution.py:23
  71.8 10.1 %collective-permute-start.21 = (bf16[128,640]{1,0:T(8,128)(2,1)S(1)}, bf16[128,640]{1,0:T(8,128)(2,1)S(1)}, u32[]{:S(2)}, u32[]{:S(2)}) collective-permute-start(bf16[128,640]{1,0:T(8,128)(2,1)S(1)} %get-tuple-element.130), channel_id=1, source_target_pairs={{0,4},{2,6},{4,8},{6,10},{8,12},{10,14},{12,16},{14,18},{16,20},{1... | collective-permute-start | bytes 491528 | tf_op jit(solution)/shard_map/ppermute | solution.py:23
  75.7 11.6 %collective-permute-start.18 = (bf16[192,1024]{1,0:T(8,128)(2,1)S(1)}, bf16[192,1024]{1,0:T(8,128)(2,1)S(1)}, u32[]{:S(2)}, u32[]{:S(2)}) collective-permute-start(bf16[192,1024]{1,0:T(8,128)(2,1)S(1)} %mixed_sent.1), channel_id=1, source_target_pairs={{0,1},{1,0},{2,3},{3,2},{4,5},{5,4},{6,7},{7,6},{8,9},{9,8},{10,11... | collective-permute-start | bytes 1179656 | tf_op jit(solution)/shard_map/ppermute | solution.py:23
  82.2 9.1 %collective-permute-start.22 = (bf16[192,640]{1,0:T(8,128)(2,1)S(1)}, bf16[192,640]{1,0:T(8,128)(2,1)S(1)}, u32[]{:S(2)}, u32[]{:S(2)}) collective-permute-start(bf16[192,640]{1,0:T(8,128)(2,1)S(1)} %grad_sent.3), channel_id=1, source_target_pairs={{0,1},{1,0},{2,3},{3,2},{4,5},{5,4},{6,7},{7,6},{8,9},{9,8},{10,11... | collective-permute-start | bytes 737288 | tf_op jit(solution)/shard_map/ppermute | solution.py:23

commit v2 on v1

--- a/solution.py
+++ b/solution.py
@@ -361,11 +361,11 @@
         scale=BUSY,
     )
     first_rows = to_groups(rows)
+    weight_outs = weights(0, ())
     expert_out = to_groups(run(whole_rows, rows_shape, [kept, arrived], 0, "expert_out_rows"))
-    weight_outs = weights(0, ())
 
     half_shape = [shape(cap, half)] * lists
-    sent = scatter(kernel(scatter_rows), oth_rows, first_rows, [], BF16, "grad_sent")
+    sent = scatter(kernel(scatter_rows), oth_rows, first_rows, [], BF16, "grad_sent", SHARED)
     first_arrived = shifted(sent, "dp", 1)
     second_rows = to_groups(run(whole_rows, half_shape, [second_kept, second_arrived], 0, "input_grad_rows"))
     first_kept = scatter(kernel(scatter_rows), own_rows, first_rows, [], F32, "grad_kept")

time: 93.3 us -> 92.8 us (level); the launches traced: 92 us -> 92.6 us
  starting transfers between devices: 32.9 us -> 34.1 us
    ppermute x23, starting transfers between devices: 32.9 us -> 34.1 us  [shifted(): return lax.ppermute(value, axis, pairs)]
  transfers between devices with their start and end apart: 23 -> 23, of which waited for: 13 -> 12; matrix products, arithmetic and copies ran while one was open for 1% -> 1% of each run, Pallas kernels for 22% -> 22%
where the time goes in v2:
time: 92.8 us; the launch traced here: 92.6 us
  starting transfers between devices  34.1 us (37%)
  waiting for transfers between devices  34 us (37%)
  Pallas kernels  20.8 us (22%)
  local copies, waits for them, and re-layouts  2.72 us (3%)
    ppermute x23, starting transfers between devices, shifted(): return lax.ppermute(value, axis, pairs)  34.1 us
    ppermute x23, waiting for transfers between devices, shifted(): return lax.ppermute(value, axis, pairs)  34 us
    pallas_call x24, Pallas kernels, run(): pl.pallas_call((lambda *refs: kernel(*refs[skipped:])) if skipped else ke...  20.8 us
    slice x5, local copies, waits for them, and re-layouts, on_device(): pieces.append((after(source, pieces[-1]) if pieces else source)[:, span(c)])  2.15 us
  transfers between devices with their start and end apart: 23, of which 12 were waited for; matrix products, arithmetic and copies ran while one was open for 1% of the time, Pallas kernels for 22%

profile of v2, /device:TPU:0, one launch (start us, length us, event | category | flops | bytes accessed | tf_op | source)
XLA Modules:
  0.0 92.6 jit_solution(3279608997702730457)
XLA Ops:
  0.7 1.1 %slice.12 = bf16[192,1024]{1,0:T(8,128)(2,1)S(1)} slice(bf16[192,2048]{1,0:T(8,128)(2,1)} %own.5), slice={[0:192], [0:1024]} | slice | bytes 786432 | tf_op jit(solution)/shard_map/slice | solution.py:307
  1.8 3.0 %collective-permute-start.1 = (bf16[192,1024]{1,0:T(8,128)(2,1)S(1)}, bf16[192,1024]{1,0:T(8,128)(2,1)S(1)}, u32[]{:S(2)}, u32[]{:S(2)}) collective-permute-start(bf16[192,1024]{1,0:T(8,128)(2,1)S(1)} %slice.12), channel_id=1, source_target_pairs={{0,1},{1,0},{2,3},{3,2},{4,5},{5,4},{6,7},{7,6},{8,9},{9,8},{10,11... | collective-permute-start | bytes 1179656 | tf_op jit(solution)/shard_map/ppermute | solution.py:23
  4.8 1.0 %slice.13 = bf16[192,1024]{1,0:T(8,128)(2,1)S(1)} slice(bf16[192,2048]{1,0:T(8,128)(2,1)} %own.5), slice={[0:192], [1024:2048]} | slice | bytes 786432 | tf_op jit(solution)/shard_map/slice | solution.py:307
  6.3 8.5 %collective-permute-done.1.oth = bf16[192,1024]{1,0:T(8,128)(2,1)S(1)} collective-permute-done((bf16[192,1024]{1,0:T(8,128)(2,1)S(1)}, bf16[192,1024]{1,0:T(8,128)(2,1)S(1)}, u32[]{:S(2)}, u32[]{:S(2)}) %collective-permute-start.1) | collective-permute-done | bytes 393248 | tf_op jit(solution)/shard_map/ppermute | solution.py:23
  15.4 2.5 %collective-permute-start.3 = (bf16[128,1024]{1,0:T(8,128)(2,1)S(1)}, bf16[128,1024]{1,0:T(8,128)(2,1)S(1)}, u32[]{:S(2)}, u32[]{:S(2)}) collective-permute-start(bf16[128,1024]{1,0:T(8,128)(2,1)S(1)} %get-tuple-element.79), channel_id=1, source_target_pairs={{0,30},{2,0},{4,2},{6,4},{8,6},{10,8},{12,10},{14,12},{16,14},{18,... | collective-permute-start | bytes 786440 | tf_op jit(solution)/shard_map/ppermute | solution.py:23
  17.9 1.6 %collective-permute-start.2 = (bf16[208,1024]{1,0:T(8,128)(2,1)S(1)}, bf16[208,1024]{1,0:T(8,128)(2,1)S(1)}, u32[]{:S(2)}, u32[]{:S(2)}) collective-permute-start(bf16[208,1024]{1,0:T(8,128)(2,1)S(1)} %fusion.1), channel_id=1, source_target_pairs={{0,1},{1,0},{2,3},{3,2},{4,5},{5,4},{6,7},{7,6},{8,9},{9,8},{10,11... | collective-permute-start | bytes 1277960 | tf_op jit(solution)/shard_map/ppermute | solution.py:23
  19.5 2.6 %collective-permute-start.4 = (bf16[128,1024]{1,0:T(8,128)(2,1)S(1)}, bf16[128,1024]{1,0:T(8,128)(2,1)S(1)}, u32[]{:S(2)}, u32[]{:S(2)}) collective-permute-start(bf16[128,1024]{1,0:T(8,128)(2,1)S(1)} %get-tuple-element.80), channel_id=1, source_target_pairs={{0,28},{2,30},{4,0},{6,2},{8,4},{10,6},{12,8},{14,10},{16,12},{18,... | collective-permute-start | bytes 786440 | tf_op jit(solution)/shard_map/ppermute | solution.py:23
  23.8 2.5 %collective-permute-start.5 = (bf16[128,1024]{1,0:T(8,128)(2,1)S(1)}, bf16[128,1024]{1,0:T(8,128)(2,1)S(1)}, u32[]{:S(2)}, u32[]{:S(2)}) collective-permute-start(bf16[128,1024]{1,0:T(8,128)(2,1)S(1)} %get-tuple-element.85), channel_id=1, source_target_pairs={{0,30},{2,0},{4,2},{6,4},{8,6},{10,8},{12,10},{14,12},{16,14},{18,... | collective-permute-start | bytes 786440 | tf_op jit(solution)/shard_map/ppermute | solution.py:23
  26.3 2.7 %collective-permute-start.6 = (bf16[128,1024]{1,0:T(8,128)(2,1)S(1)}, bf16[128,1024]{1,0:T(8,128)(2,1)S(1)}, u32[]{:S(2)}, u32[]{:S(2)}) collective-permute-start(bf16[128,1024]{1,0:T(8,128)(2,1)S(1)} %get-tuple-element.86), channel_id=1, source_target_pairs={{0,28},{2,30},{4,0},{6,2},{8,4},{10,6},{12,8},{14,10},{16,12},{18,... | collective-permute-start | bytes 786440 | tf_op jit(solution)/shard_map/ppermute | solution.py:23
  30.0 2.3 %collective-permute-done.2.oth.oth_gate.gate = bf16[208,1024]{1,0:T(8,128)(2,1)S(1)} collective-permute-done((bf16[208,1024]{1,0:T(8,128)(2,1)S(1)}, bf16[208,1024]{1,0:T(8,128)(2,1)S(1)}, u32[]{:S(2)}, u32[]{:S(2)}) %collective-permute-start.2) | collective-permute-done | bytes 426016 | tf_op jit(solution)/shard_map/ppermute | solution.py:23
  33.0 2.5 %collective-permute-start.8 = (bf16[128,1024]{1,0:T(8,128)(2,1)S(1)}, bf16[128,1024]{1,0:T(8,128)(2,1)S(1)}, u32[]{:S(2)}, u32[]{:S(2)}) collective-permute-start(bf16[128,1024]{1,0:T(8,128)(2,1)S(1)} %get-tuple-element.96), channel_id=1, source_target_pairs={{0,30},{2,0},{4,2},{6,4},{8,6},{10,8},{12,10},{14,12},{16,14},{18,... | collective-permute-start | bytes 786440 | tf_op jit(solution)/shard_map/ppermute | solution.py:23
  35.6 2.7 %collective-permute-start.9 = (bf16[128,1024]{1,0:T(8,128)(2,1)S(1)}, bf16[128,1024]{1,0:T(8,128)(2,1)S(1)}, u32[]{:S(2)}, u32[]{:S(2)}) collective-permute-start(bf16[128,1024]{1,0:T(8,128)(2,1)S(1)} %get-tuple-element.97), channel_id=1, source_target_pairs={{0,28},{2,30},{4,0},{6,2},{8,4},{10,6},{12,8},{14,10},{16,12},{18,... | collective-permute-start | bytes 786440 | tf_op jit(solution)/shard_map/ppermute | solution.py:23
  38.2 1.2 %hidden.1 = (bf16[384,384]{1,0:T(8,128)(2,1)S(1)}, f32[384,384]{1,0:T(8,128)S(1)}, f32[384,384]{1,0:T(8,128)S(1)}) custom-call(bf16[128,1024]{1,0:T(8,128)(2,1)S(1)} %get-tuple-element.133.refs_0_.refs_3_, bf16[128,1024]{1,0:T(8,128)(2,1)S(1)} %collective-permute-done.5.refs_1_.refs_4_, bf16[128,1024]{1,0:T(8,128)(2,1)S(1)} %collective-permute-done.6.refs_2_.refs_5_, ...), custom_call_target="tpu_custom_call" | custom-call | flops 6039797 | bytes 38338 | tf_op jit(solution)/shard_map/hidden/pallas_call | solution.py:65
  40.6 1.6 %collective-permute-start.12 = (bf16[384,1024]{1,0:T(8,128)(2,1)S(1)}, bf16[384,1024]{1,0:T(8,128)(2,1)S(1)}, u32[]{:S(2)}, u32[]{:S(2)}) collective-permute-start(bf16[384,1024]{1,0:T(8,128)(2,1)S(1)} %get-tuple-element.92), channel_id=1, source_target_pairs={{0,1},{1,0},{2,3},{3,2},{4,5},{5,4},{6,7},{7,6},{8,9},{9,8},{10,11... | collective-permute-start | bytes 2359304 | tf_op jit(solution)/shard_map/ppermute | solution.py:23
  42.9 1.7 %collective-permute-start.10 = (bf16[128,1024]{1,0:T(8,128)(2,1)S(1)}, bf16[128,1024]{1,0:T(8,128)(2,1)S(1)}, u32[]{:S(2)}, u32[]{:S(2)}) collective-permute-start(bf16[128,1024]{1,0:T(8,128)(2,1)S(1)} %get-tuple-element.99), channel_id=1, source_target_pairs={{0,30},{2,0},{4,2},{6,4},{8,6},{10,8},{12,10},{14,12},{16,14},{18,... | collective-permute-start | bytes 786440 | tf_op jit(solution)/shard_map/ppermute | solution.py:23
  44.6 1.3 %collective-permute-start.11 = (bf16[128,1024]{1,0:T(8,128)(2,1)S(1)}, bf16[128,1024]{1,0:T(8,128)(2,1)S(1)}, u32[]{:S(2)}, u32[]{:S(2)}) collective-permute-start(bf16[128,1024]{1,0:T(8,128)(2,1)S(1)} %get-tuple-element.100), channel_id=1, source_target_pairs={{0,28},{2,30},{4,0},{6,2},{8,4},{10,6},{12,8},{14,10},{16,12},{18,... | collective-permute-start | bytes 786440 | tf_op jit(solution)/shard_map/ppermute | solution.py:23
  46.4 4.2 %collective-permute-done.10.refs_1_.refs_7_ = bf16[128,1024]{1,0:T(8,128)(2,1)S(1)} collective-permute-done((bf16[128,1024]{1,0:T(8,128)(2,1)S(1)}, bf16[128,1024]{1,0:T(8,128)(2,1)S(1)}, u32[]{:S(2)}, u32[]{:S(2)}) %collective-permute-start.10) | collective-permute-done | bytes 262176 | tf_op jit(solution)/shard_map/ppermute | solution.py:23
  50.6 3.9 %collective-permute-done.11.refs_2_.refs_8_ = bf16[128,1024]{1,0:T(8,128)(2,1)S(1)} collective-permute-done((bf16[128,1024]{1,0:T(8,128)(2,1)S(1)}, bf16[128,1024]{1,0:T(8,128)(2,1)S(1)}, u32[]{:S(2)}, u32[]{:S(2)}) %collective-permute-start.11) | collective-permute-done | bytes 262176 | tf_op jit(solution)/shard_map/ppermute | solution.py:23
  55.2 1.4 %input_grad.2 = (bf16[384,640]{1,0:T(8,128)(2,1)S(1)}, f32[384,640]{1,0:T(8,128)S(1)}) custom-call(s32[1,1]{1,0:T(1,128)} %bitcast.3.me, bf16[384,384]{1,0:T(8,128)(2,1)S(1)} %get-tuple-element.107.gate_grad.refs_7_.refs_10_, bf16[384,384]{1,0:T(8,128)(2,1)S(1)} %get-tuple-element.105.up_grad.refs_8_.refs_11_, bf16[2048,384]{1,0:T(8,128)(2,1)S(1)} %bitcast.36, ...), custom_call_target="tpu_custom_call" | custom-call | flops 9059696640 | bytes 35389460 | tf_op jit(solution)/shard_map/input_grad/pallas_call | solution.py:65
  58.0 1.6 %collective-permute-start.16 = (bf16[144,768]{1,0:T(8,128)(2,1)S(1)}, bf16[144,768]{1,0:T(8,128)(2,1)S(1)}, u32[]{:S(2)}, u32[]{:S(2)}) collective-permute-start(bf16[144,768]{1,0:T(8,128)(2,1)S(1)} %get-tuple-element.117), channel_id=1, source_target_pairs={{0,4},{2,6},{4,8},{6,10},{8,12},{10,14},{12,16},{14,18},{16,20},{1... | collective-permute-start | bytes 663560 | tf_op jit(solution)/shard_map/ppermute | solution.py:23
  59.6 2.4 %w_grads.2 = (bf16[2048,384]{1,0:T(8,128)(2,1)}, bf16[2048,384]{1,0:T(8,128)(2,1)}, bf16[384,2048]{1,0:T(8,128)(2,1)}) custom-call(bf16[128,1024]{1,0:T(8,128)(2,1)S(1)} %get-tuple-element.110.refs_0_, bf16[128,1024]{1,0:T(8,128)(2,1)S(1)} %collective-permute-done.3.refs_1_, bf16[128,1024]{1,0:T(8,128)(2,1)S(1)} %collective-permute-done.4.refs_2_, ...), custom_call_target="tpu_custom_call" | custom-call | flops 9059696 | bytes 48168 | tf_op jit(solution)/shard_map/w_grads/pallas_call | solution.py:65
  62.2 1.5 %collective-permute-start.14 = (bf16[128,1024]{1,0:T(8,128)(2,1)S(1)}, bf16[128,1024]{1,0:T(8,128)(2,1)S(1)}, u32[]{:S(2)}, u32[]{:S(2)}) collective-permute-start(bf16[128,1024]{1,0:T(8,128)(2,1)S(1)} %get-tuple-element.115), channel_id=1, source_target_pairs={{0,4},{2,6},{4,8},{6,10},{8,12},{10,14},{12,16},{14,18},{16,20},{1... | collective-permute-start | bytes 786440 | tf_op jit(solution)/shard_map/ppermute | solution.py:23
  63.7 1.4 %collective-permute-start.13 = (bf16[128,1024]{1,0:T(8,128)(2,1)S(1)}, bf16[128,1024]{1,0:T(8,128)(2,1)S(1)}, u32[]{:S(2)}, u32[]{:S(2)}) collective-permute-start(bf16[128,1024]{1,0:T(8,128)(2,1)S(1)} %get-tuple-element.114), channel_id=1, source_target_pairs={{0,2},{2,4},{4,6},{6,8},{8,10},{10,12},{12,14},{14,16},{16,18},{18... | collective-permute-start | bytes 786440 | tf_op jit(solution)/shard_map/ppermute | solution.py:23
  65.1 4.0 %collective-permute-done.16.refs_2_ = bf16[144,768]{1,0:T(8,128)(2,1)S(1)} collective-permute-done((bf16[144,768]{1,0:T(8,128)(2,1)S(1)}, bf16[144,768]{1,0:T(8,128)(2,1)S(1)}, u32[]{:S(2)}, u32[]{:S(2)}) %collective-permute-start.16) | collective-permute-done | bytes 221216 | tf_op jit(solution)/shard_map/ppermute | solution.py:23
  72.4 2.3 %collective-permute-done.14.refs_2_.refs_5_ = bf16[128,1024]{1,0:T(8,128)(2,1)S(1)} collective-permute-done((bf16[128,1024]{1,0:T(8,128)(2,1)S(1)}, bf16[128,1024]{1,0:T(8,128)(2,1)S(1)}, u32[]{:S(2)}, u32[]{:S(2)}) %collective-permute-start.14) | collective-permute-done | bytes 262176 | tf_op jit(solution)/shard_map/ppermute | solution.py:23
  74.7 3.2 %collective-permute-done.13.refs_1_.refs_4_ = bf16[128,1024]{1,0:T(8,128)(2,1)S(1)} collective-permute-done((bf16[128,1024]{1,0:T(8,128)(2,1)S(1)}, bf16[128,1024]{1,0:T(8,128)(2,1)S(1)}, u32[]{:S(2)}, u32[]{:S(2)}) %collective-permute-start.13) | collective-permute-done | bytes 262176 | tf_op jit(solution)/shard_map/ppermute | solution.py:23
  78.5 1.1 %collective-permute-start.18 = (bf16[192,1024]{1,0:T(8,128)(2,1)S(1)}, bf16[192,1024]{1,0:T(8,128)(2,1)S(1)}, u32[]{:S(2)}, u32[]{:S(2)}) collective-permute-start(bf16[192,1024]{1,0:T(8,128)(2,1)S(1)} %mixed_sent.1), channel_id=1, source_target_pairs={{0,1},{1,0},{2,3},{3,2},{4,5},{5,4},{6,7},{7,6},{8,9},{9,8},{10,11... | collective-permute-start | bytes 1179656 | tf_op jit(solution)/shard_map/ppermute | solution.py:23
  79.6 1.3 %mixed_own.1.refs_1_ = bf16[192,2048]{1,0:T(8,128)(2,1)} custom-call(s32[1]{0:T(128)} %bitcast.1.refs_0_, s32[384,1]{1,0:T(8,128)S(1)} %bitcast.33, f32[3,192]{1,0:T(4,128)S(1)} %bitcast_convert_fusion.own_gate.refs_2_.gate, bf16[128,1024]{1,0:T(8,128)(2,1)S(1)} %get-tuple-element.113.refs_0_.refs_3_, ...), custom_call_target="tpu_custom_call" | custom-call | flops 1509949 | bytes 11815 | tf_op jit(solution)/shard_map/mixed_own/pallas_call | solution.py:65
  82.2 1.5 %collective-permute-start.22 = (bf16[192,640]{1,0:T(8,128)(2,1)S(1)}, bf16[192,640]{1,0:T(8,128)(2,1)S(1)}, u32[]{:S(2)}, u32[]{:S(2)}) collective-permute-start(bf16[192,640]{1,0:T(8,128)(2,1)S(1)} %grad_sent.3), channel_id=1, source_target_pairs={{0,1},{1,0},{2,3},{3,2},{4,5},{5,4},{6,7},{7,6},{8,9},{9,8},{10,11... | collective-permute-start | bytes 737288 | tf_op jit(solution)/shard_map/ppermute | solution.py:23
  83.7 1.0 %grad_own.1.refs_1_ = bf16[192,2048]{1,0:T(8,128)(2,1)} custom-call(s32[1]{0:T(128)} %bitcast.1.refs_0_, bf16[192,2048]{1,0:T(8,128)(2,1)} %get-tuple-element.128.refs_1_, s32[3,128]{1,0:T(4,128)S(1)} %get-tuple-element.141.rows.refs_2_, bf16[128,640]{1,0:T(8,128)(2,1)S(1)} %get-tuple-element.121.refs_0_.refs_3_, ...), custom_call_target="tpu_custom_call", output_to_operand_aliasing={{}: (1, {})} | custom-call | flops 943718400 | bytes 7380480 | tf_op jit(solution)/shard_map/grad_own/pallas_call | solution.py:65
  84.7 2.6 %w_grads.3 = (bf16[2048,384]{1,0:T(8,128)(2,1)}, bf16[2048,384]{1,0:T(8,128)(2,1)}, bf16[384,2048]{1,0:T(8,128)(2,1)}) custom-call(bf16[2048,384]{1,0:T(8,128)(2,1)} %get-tuple-element.111.refs_0_, bf16[2048,384]{1,0:T(8,128)(2,1)} %get-tuple-element.125.refs_1_, ...), custom_call_target="tpu_custom_call", output_to_operand_aliasing={{0}: (0, {}), {1}: (1, {}), {2}: (2, {})} | custom-call | flops 9059696 | bytes 48168 | tf_op jit(solution)/shard_map/w_grads/pallas_call | solution.py:65
  88.1 3.8 %collective-permute-done.22.refs_2_ = bf16[192,640]{1,0:T(8,128)(2,1)S(1)} collective-permute-done((bf16[192,640]{1,0:T(8,128)(2,1)S(1)}, bf16[192,640]{1,0:T(8,128)(2,1)S(1)}, u32[]{:S(2)}, u32[]{:S(2)}) %collective-permute-start.22) | collective-permute-done | bytes 245792 | tf_op jit(solution)/shard_map/ppermute | solution.py:23
  (64 shorter events, 15.9 us)
Async XLA Ops:
  0.6 14.1 %copy-start = (bf16[192,2048]{1,0:T(8,128)(2,1)S(1)}, bf16[192,2048]{1,0:T(8,128)(2,1)}, u32[]{:S(2)}) copy-start(bf16[192,2048]{1,0:T(8,128)(2,1)} %own.5) | copy-start | bytes 2359300
  0.6 5.3 %copy-start.6 = (s32[3,128]{1,0:T(4,128)S(1)}, s32[3,128]{1,0:T(4,128)}, u32[]{:S(2)}) copy-start(s32[3,128]{1,0:T(4,128)} %param.10) | copy-start | bytes 4612
  1.8 13.0 %collective-permute-start.1 = (bf16[192,1024]{1,0:T(8,128)(2,1)S(1)}, bf16[192,1024]{1,0:T(8,128)(2,1)S(1)}, u32[]{:S(2)}, u32[]{:S(2)}) collective-permute-start(bf16[192,1024]{1,0:T(8,128)(2,1)S(1)} %slice.12), channel_id=1, source_target_pairs={{0,1},{1,0},{2,3},{3,2},{4,5},{5,4},{6,7},{7,6},{8,9},{9,8},{10,11... | collective-permute-start | bytes 1179656 | tf_op jit(solution)/shard_map/ppermute | solution.py:23
  5.8 12.1 %slice-start = ((bf16[192,2048]{1,0:T(8,128)(2,1)}), bf16[192,1024]{1,0:T(8,128)(2,1)S(1)}, s32[]{:S(2)}) async-start(bf16[192,2048]{1,0:T(8,128)(2,1)} %own.7), calls=%async_computation | async-start | bytes 786432 | tf_op jit(solution)/shard_map/slice | solution.py:307
  5.8 12.1 %copy-start.5 = (bf16[192,3]{0,1:T(4,128)(2,1)S(1)}, bf16[192,3]{0,1:T(4,128)(2,1)}, u32[]{:S(2)}) copy-start(bf16[192,3]{0,1:T(4,128)(2,1)} %param.9) | copy-start | bytes 3460
  5.8 17.3 %collective-permute-start = (bf16[192,1024]{1,0:T(8,128)(2,1)S(1)}, bf16[192,1024]{1,0:T(8,128)(2,1)S(1)}, u32[]{:S(2)}, u32[]{:S(2)}) collective-permute-start(bf16[192,1024]{1,0:T(8,128)(2,1)S(1)} %slice.13), channel_id=1, source_target_pairs={{0,1},{1,0},{2,3},{3,2},{4,5},{5,4},{6,7},{7,6},{8,9},{9,8},{10,11... | collective-permute-start | bytes 1179656 | tf_op jit(solution)/shard_map/ppermute | solution.py:23
  6.3 15.9 %copy-start.1 = (bf16[192,2048]{1,0:T(8,128)(2,1)S(1)}, bf16[192,2048]{1,0:T(8,128)(2,1)}, u32[]{:S(2)}) copy-start(bf16[192,2048]{1,0:T(8,128)(2,1)} %own.7) | copy-start | bytes 2359300
  15.4 11.0 %collective-permute-start.3 = (bf16[128,1024]{1,0:T(8,128)(2,1)S(1)}, bf16[128,1024]{1,0:T(8,128)(2,1)S(1)}, u32[]{:S(2)}, u32[]{:S(2)}) collective-permute-start(bf16[128,1024]{1,0:T(8,128)(2,1)S(1)} %get-tuple-element.79), channel_id=1, source_target_pairs={{0,30},{2,0},{4,2},{6,4},{8,6},{10,8},{12,10},{14,12},{16,14},{18,... | collective-permute-start | bytes 786440 | tf_op jit(solution)/shard_map/ppermute | solution.py:23
  17.9 11.1 %copy-start.2 = (bf16[1,2048,384]{2,1,0:T(8,128)(2,1)S(1)}, bf16[1,2048,384]{2,1,0:T(8,128)(2,1)}, u32[]{:S(2)}) copy-start(bf16[1,2048,384]{2,1,0:T(8,128)(2,1)} %param.11) | copy-start | bytes 4718596
  17.9 11.1 %copy-start.3 = (bf16[1,2048,384]{2,1,0:T(8,128)(2,1)S(1)}, bf16[1,2048,384]{2,1,0:T(8,128)(2,1)}, u32[]{:S(2)}) copy-start(bf16[1,2048,384]{2,1,0:T(8,128)(2,1)} %param.12) | copy-start | bytes 4718596
  17.9 14.3 %collective-permute-start.2 = (bf16[208,1024]{1,0:T(8,128)(2,1)S(1)}, bf16[208,1024]{1,0:T(8,128)(2,1)S(1)}, u32[]{:S(2)}, u32[]{:S(2)}) collective-permute-start(bf16[208,1024]{1,0:T(8,128)(2,1)S(1)} %fusion.1), channel_id=1, source_target_pairs={{0,1},{1,0},{2,3},{3,2},{4,5},{5,4},{6,7},{7,6},{8,9},{9,8},{10,11... | collective-permute-start | bytes 1277960 | tf_op jit(solution)/shard_map/ppermute | solution.py:23
  19.5 9.4 %collective-permute-start.4 = (bf16[128,1024]{1,0:T(8,128)(2,1)S(1)}, bf16[128,1024]{1,0:T(8,128)(2,1)S(1)}, u32[]{:S(2)}, u32[]{:S(2)}) collective-permute-start(bf16[128,1024]{1,0:T(8,128)(2,1)S(1)} %get-tuple-element.80), channel_id=1, source_target_pairs={{0,28},{2,30},{4,0},{6,2},{8,4},{10,6},{12,8},{14,10},{16,12},{18,... | collective-permute-start | bytes 786440 | tf_op jit(solution)/shard_map/ppermute | solution.py:23
  22.2 20.0 %collective-permute-start.7 = (bf16[192,1024]{1,0:T(8,128)(2,1)S(1)}, bf16[192,1024]{1,0:T(8,128)(2,1)S(1)}, u32[]{:S(2)}, u32[]{:S(2)}) collective-permute-start(bf16[192,1024]{1,0:T(8,128)(2,1)S(1)} %slice.15), channel_id=1, source_target_pairs={{0,1},{1,0},{2,3},{3,2},{4,5},{5,4},{6,7},{7,6},{8,9},{9,8},{10,11... | collective-permute-start | bytes 1179656 | tf_op jit(solution)/shard_map/ppermute | solution.py:23
  23.8 14.4 %collective-permute-start.5 = (bf16[128,1024]{1,0:T(8,128)(2,1)S(1)}, bf16[128,1024]{1,0:T(8,128)(2,1)S(1)}, u32[]{:S(2)}, u32[]{:S(2)}) collective-permute-start(bf16[128,1024]{1,0:T(8,128)(2,1)S(1)} %get-tuple-element.85), channel_id=1, source_target_pairs={{0,30},{2,0},{4,2},{6,4},{8,6},{10,8},{12,10},{14,12},{16,14},{18,... | collective-permute-start | bytes 786440 | tf_op jit(solution)/shard_map/ppermute | solution.py:23
  26.3 11.9 %collective-permute-start.6 = (bf16[128,1024]{1,0:T(8,128)(2,1)S(1)}, bf16[128,1024]{1,0:T(8,128)(2,1)S(1)}, u32[]{:S(2)}, u32[]{:S(2)}) collective-permute-start(bf16[128,1024]{1,0:T(8,128)(2,1)S(1)} %get-tuple-element.86), channel_id=1, source_target_pairs={{0,28},{2,30},{4,0},{6,2},{8,4},{10,6},{12,8},{14,10},{16,12},{18,... | collective-permute-start | bytes 786440 | tf_op jit(solution)/shard_map/ppermute | solution.py:23
  33.0 12.8 %collective-permute-start.8 = (bf16[128,1024]{1,0:T(8,128)(2,1)S(1)}, bf16[128,1024]{1,0:T(8,128)(2,1)S(1)}, u32[]{:S(2)}, u32[]{:S(2)}) collective-permute-start(bf16[128,1024]{1,0:T(8,128)(2,1)S(1)} %get-tuple-element.96), channel_id=1, source_target_pairs={{0,30},{2,0},{4,2},{6,4},{8,6},{10,8},{12,10},{14,12},{16,14},{18,... | collective-permute-start | bytes 786440 | tf_op jit(solution)/shard_map/ppermute | solution.py:23
  35.6 10.3 %collective-permute-start.9 = (bf16[128,1024]{1,0:T(8,128)(2,1)S(1)}, bf16[128,1024]{1,0:T(8,128)(2,1)S(1)}, u32[]{:S(2)}, u32[]{:S(2)}) collective-permute-start(bf16[128,1024]{1,0:T(8,128)(2,1)S(1)} %get-tuple-element.97), channel_id=1, source_target_pairs={{0,28},{2,30},{4,0},{6,2},{8,4},{10,6},{12,8},{14,10},{16,12},{18,... | collective-permute-start | bytes 786440 | tf_op jit(solution)/shard_map/ppermute | solution.py:23
  38.2 1.4 %copy-start.4 = (bf16[1,384,2048]{2,1,0:T(8,128)(2,1)S(1)}, bf16[1,384,2048]{2,1,0:T(8,128)(2,1)}, u32[]{:S(2)}) copy-start(bf16[1,384,2048]{2,1,0:T(8,128)(2,1)} %param.13) | copy-start | bytes 4718596
  40.6 21.4 %collective-permute-start.12 = (bf16[384,1024]{1,0:T(8,128)(2,1)S(1)}, bf16[384,1024]{1,0:T(8,128)(2,1)S(1)}, u32[]{:S(2)}, u32[]{:S(2)}) collective-permute-start(bf16[384,1024]{1,0:T(8,128)(2,1)S(1)} %get-tuple-element.92), channel_id=1, source_target_pairs={{0,1},{1,0},{2,3},{3,2},{4,5},{5,4},{6,7},{7,6},{8,9},{9,8},{10,11... | collective-permute-start | bytes 2359304 | tf_op jit(solution)/shard_map/ppermute | solution.py:23
  42.9 7.7 %collective-permute-start.10 = (bf16[128,1024]{1,0:T(8,128)(2,1)S(1)}, bf16[128,1024]{1,0:T(8,128)(2,1)S(1)}, u32[]{:S(2)}, u32[]{:S(2)}) collective-permute-start(bf16[128,1024]{1,0:T(8,128)(2,1)S(1)} %get-tuple-element.99), channel_id=1, source_target_pairs={{0,30},{2,0},{4,2},{6,4},{8,6},{10,8},{12,10},{14,12},{16,14},{18,... | collective-permute-start | bytes 786440 | tf_op jit(solution)/shard_map/ppermute | solution.py:23
  44.6 9.9 %collective-permute-start.11 = (bf16[128,1024]{1,0:T(8,128)(2,1)S(1)}, bf16[128,1024]{1,0:T(8,128)(2,1)S(1)}, u32[]{:S(2)}, u32[]{:S(2)}) collective-permute-start(bf16[128,1024]{1,0:T(8,128)(2,1)S(1)} %get-tuple-element.100), channel_id=1, source_target_pairs={{0,28},{2,30},{4,0},{6,2},{8,4},{10,6},{12,8},{14,10},{16,12},{18,... | collective-permute-start | bytes 786440 | tf_op jit(solution)/shard_map/ppermute | solution.py:23
  56.6 15.0 %collective-permute-start.17 = (bf16[384,640]{1,0:T(8,128)(2,1)S(1)}, bf16[384,640]{1,0:T(8,128)(2,1)S(1)}, u32[]{:S(2)}, u32[]{:S(2)}) collective-permute-start(bf16[384,640]{1,0:T(8,128)(2,1)S(1)} %get-tuple-element.106), channel_id=1, source_target_pairs={{0,1},{1,0},{2,3},{3,2},{4,5},{5,4},{6,7},{7,6},{8,9},{9,8},{10,11... | collective-permute-start | bytes 1474568 | tf_op jit(solution)/shard_map/ppermute | solution.py:23
  58.0 11.1 %collective-permute-start.16 = (bf16[144,768]{1,0:T(8,128)(2,1)S(1)}, bf16[144,768]{1,0:T(8,128)(2,1)S(1)}, u32[]{:S(2)}, u32[]{:S(2)}) collective-permute-start(bf16[144,768]{1,0:T(8,128)(2,1)S(1)} %get-tuple-element.117), channel_id=1, source_target_pairs={{0,4},{2,6},{4,8},{6,10},{8,12},{10,14},{12,16},{14,18},{16,20},{1... | collective-permute-start | bytes 663560 | tf_op jit(solution)/shard_map/ppermute | solution.py:23
  59.6 10.3 %collective-permute-start.15 = (bf16[144,768]{1,0:T(8,128)(2,1)S(1)}, bf16[144,768]{1,0:T(8,128)(2,1)S(1)}, u32[]{:S(2)}, u32[]{:S(2)}) collective-permute-start(bf16[144,768]{1,0:T(8,128)(2,1)S(1)} %get-tuple-element.116), channel_id=1, source_target_pairs={{0,2},{2,4},{4,6},{6,8},{8,10},{10,12},{12,14},{14,16},{16,18},{18... | collective-permute-start | bytes 663560 | tf_op jit(solution)/shard_map/ppermute | solution.py:23
  62.2 12.5 %collective-permute-start.14 = (bf16[128,1024]{1,0:T(8,128)(2,1)S(1)}, bf16[128,1024]{1,0:T(8,128)(2,1)S(1)}, u32[]{:S(2)}, u32[]{:S(2)}) collective-permute-start(bf16[128,1024]{1,0:T(8,128)(2,1)S(1)} %get-tuple-element.115), channel_id=1, source_target_pairs={{0,4},{2,6},{4,8},{6,10},{8,12},{10,14},{12,16},{14,18},{16,20},{1... | collective-permute-start | bytes 786440 | tf_op jit(solution)/shard_map/ppermute | solution.py:23
  63.7 14.2 %collective-permute-start.13 = (bf16[128,1024]{1,0:T(8,128)(2,1)S(1)}, bf16[128,1024]{1,0:T(8,128)(2,1)S(1)}, u32[]{:S(2)}, u32[]{:S(2)}) collective-permute-start(bf16[128,1024]{1,0:T(8,128)(2,1)S(1)} %get-tuple-element.114), channel_id=1, source_target_pairs={{0,2},{2,4},{4,6},{6,8},{8,10},{10,12},{12,14},{14,16},{16,18},{18... | collective-permute-start | bytes 786440 | tf_op jit(solution)/shard_map/ppermute | solution.py:23
  70.3 10.6 %collective-permute-start.19 = (bf16[208,768]{1,0:T(8,128)(2,1)S(1)}, bf16[208,768]{1,0:T(8,128)(2,1)S(1)}, u32[]{:S(2)}, u32[]{:S(2)}) collective-permute-start(bf16[208,768]{1,0:T(8,128)(2,1)S(1)} %grad_sent.2), channel_id=1, source_target_pairs={{0,1},{1,0},{2,3},{3,2},{4,5},{5,4},{6,7},{7,6},{8,9},{9,8},{10,11... | collective-permute-start | bytes 958472 | tf_op jit(solution)/shard_map/ppermute | solution.py:23
  71.7 10.1 %collective-permute-start.20 = (bf16[128,640]{1,0:T(8,128)(2,1)S(1)}, bf16[128,640]{1,0:T(8,128)(2,1)S(1)}, u32[]{:S(2)}, u32[]{:S(2)}) collective-permute-start(bf16[128,640]{1,0:T(8,128)(2,1)S(1)} %get-tuple-element.129), channel_id=1, source_target_pairs={{0,2},{2,4},{4,6},{6,8},{8,10},{10,12},{12,14},{14,16},{16,18},{18... | collective-permute-start | bytes 491528 | tf_op jit(solution)/shard_map/ppermute | solution.py:23
  71.8 10.1 %collective-permute-start.21 = (bf16[128,640]{1,0:T(8,128)(2,1)S(1)}, bf16[128,640]{1,0:T(8,128)(2,1)S(1)}, u32[]{:S(2)}, u32[]{:S(2)}) collective-permute-start(bf16[128,640]{1,0:T(8,128)(2,1)S(1)} %get-tuple-element.130), channel_id=1, source_target_pairs={{0,4},{2,6},{4,8},{6,10},{8,12},{10,14},{12,16},{14,18},{16,20},{1... | collective-permute-start | bytes 491528 | tf_op jit(solution)/shard_map/ppermute | solution.py:23
  78.5 8.8 %collective-permute-start.18 = (bf16[192,1024]{1,0:T(8,128)(2,1)S(1)}, bf16[192,1024]{1,0:T(8,128)(2,1)S(1)}, u32[]{:S(2)}, u32[]{:S(2)}) collective-permute-start(bf16[192,1024]{1,0:T(8,128)(2,1)S(1)} %mixed_sent.1), channel_id=1, source_target_pairs={{0,1},{1,0},{2,3},{3,2},{4,5},{5,4},{6,7},{7,6},{8,9},{9,8},{10,11... | collective-permute-start | bytes 1179656 | tf_op jit(solution)/shard_map/ppermute | solution.py:23
  82.2 9.7 %collective-permute-start.22 = (bf16[192,640]{1,0:T(8,128)(2,1)S(1)}, bf16[192,640]{1,0:T(8,128)(2,1)S(1)}, u32[]{:S(2)}, u32[]{:S(2)}) collective-permute-start(bf16[192,640]{1,0:T(8,128)(2,1)S(1)} %grad_sent.3), channel_id=1, source_target_pairs={{0,1},{1,0},{2,3},{3,2},{4,5},{5,4},{6,7},{7,6},{8,9},{9,8},{10,11... | collective-permute-start | bytes 737288 | tf_op jit(solution)/shard_map/ppermute | solution.py:23
